TPU v7x, 256 devices: a whole 4x4x8 slice. The times are simulated.
256 devices in a mesh: tm: 64 (over x_hi, y, z), height: 4 (over x_lo, core).
Axes of the slice: x: 4 (x_hi: 2, x_lo: 2; x = x_hi * 2 + x_lo), y: 4, z: 8, core: 2. Of those that a mesh axis runs over, the one named last changes fastest.
Arguments:
- query_states: bfloat16 [128, 64, 16, 1536], P('tm', 'height'), may hold values from -9 to 9
- key_states: bfloat16 [128, 64, 16, 1536], P('tm', 'height'), may hold values from -9 to 9
- value_states: bfloat16 [128, 64, 16, 1536], P('tm', 'height'), may hold values from -6 to 6
- shifts: int32 [2], replicated, may hold values from 1 to 7
- conv_kernel: float32 [27, 1536], replicated, may hold values from -0.5 to 0.5
- out_weight: bfloat16 [1536, 3072], replicated, may hold values from -0.15625 to 0.15625
Outputs:
- block_out: bfloat16 [128, 64, 16, 3072], P('tm', 'height')
All inputs are finite; a program needn't handle non-finite values.
Results may differ from a plain program's by a relative error of at most 0.0059.
Values may be sent and summed in bfloat16 or wider, within the bound.
A program may use at most 192 MiB of HBM per device.

v0:
```python
import math

import jax
import jax.numpy as jnp
from jax import lax
from jax.sharding import PartitionSpec as P

HEAD_DIM = 128


def shifted(value, axis, steps):
    count = lax.axis_size(axis)
    pairs = [(source, (source + steps) % count) for source in range(count)]
    return lax.ppermute(value, axis, pairs)


def with_halo(cells, sides, width):
    for axis, dim in sides:
        count = lax.axis_size(axis)
        ends = count - 1
        head = lax.slice_in_dim(cells, 0, width, axis=dim)
        tail = lax.slice_in_dim(cells, cells.shape[dim] - width, cells.shape[dim], axis=dim)
        cells = jnp.concatenate(
            [
                lax.ppermute(tail, axis, [(i, (i + 1) % count) for i in range(ends)]),
                cells,
                lax.ppermute(head, axis, [((i + 1) % count, i) for i in range(ends)]),
            ],
            axis=dim,
        )
    return cells


def soft_weights(scores):
    row_max = jnp.max(scores, axis=-1, keepdims=True)
    spread = jnp.exp(scores - row_max)
    return (spread / jnp.sum(spread, axis=-1, keepdims=True)).astype(jnp.bfloat16)


def conv_local(rim_values, conv_kernel):
    frame_count = rim_values.shape[0] - 2
    row_count = rim_values.shape[1] - 2
    col_count = rim_values.shape[2]
    padded = jnp.pad(rim_values, ((0, 0), (0, 0), (1, 1), (0, 0)))
    summed = jnp.zeros((frame_count, row_count, col_count, rim_values.shape[3]), jnp.float32)
    for offset in range(27):
        delta_t, delta_r, delta_c = (offset // 9, offset // 3 % 3, offset % 3)
        slab = padded[
            delta_t : delta_t + frame_count,
            delta_r : delta_r + row_count,
            delta_c : delta_c + col_count,
        ]
        summed = summed + conv_kernel[offset] * slab.astype(jnp.float32)
    return summed


def attend_windows(query_block, key_block, value_block):
    row_count, col_count, channels = (
        query_block.shape[1],
        query_block.shape[2],
        query_block.shape[3],
    )
    local_heads = channels // HEAD_DIM

    def window_tokens(values):
        values = values.reshape(2, row_count // 8, 8, col_count // 8, 8, local_heads, HEAD_DIM)
        return values.transpose(1, 3, 5, 0, 2, 4, 6).reshape(
            row_count // 8, col_count // 8, local_heads, 128, HEAD_DIM
        )

    scores = jnp.einsum(
        "awhqd,awhkd->awhqk",
        window_tokens(query_block),
        window_tokens(key_block),
        preferred_element_type=jnp.float32,
    ) * (1.0 / math.sqrt(HEAD_DIM))
    weights = soft_weights(scores)
    result = jnp.einsum(
        "awhqk,awhkd->awhqd",
        weights,
        window_tokens(value_block),
        preferred_element_type=jnp.float32,
    ).astype(jnp.bfloat16)
    result = result.reshape(row_count // 8, col_count // 8, local_heads, 2, 8, 8, HEAD_DIM)
    return result.transpose(3, 0, 4, 1, 5, 2, 6).reshape(2, row_count, col_count, channels)


def pair_attend(selected):
    partner = shifted(selected[:, 0], "tm", -1)
    paired = jnp.stack([selected[:, 1], partner], axis=1)
    result = attend_windows(paired[0], paired[1], paired[2])
    returned = shifted(result[1], "tm", 1)
    return jnp.stack([returned, result[0]])


def body(query_states, key_states, value_states, shifts, conv_kernel, out_weight):
    shift_rows, shift_cols = (shifts[0], shifts[1])
    frame_count, row_count, col_count, channels = query_states.shape
    rim_values = with_halo(value_states, (("tm", 0), ("height", 1)), 1)
    position_term = conv_local(rim_values, conv_kernel)
    stacked = jnp.stack([query_states, key_states, value_states])
    below_rows = shifted(stacked, "height", -1)
    selected = lax.dynamic_slice_in_dim(
        jnp.concatenate([stacked, below_rows], axis=2), shift_rows, row_count, 2
    )
    selected = jnp.roll(selected, -shift_cols, axis=3)
    attended = pair_attend(selected)
    attended = jnp.roll(attended, shift_cols, axis=2)
    above_rows = shifted(attended, "height", 1)
    settled = lax.dynamic_slice_in_dim(
        jnp.concatenate([above_rows, attended], axis=1), row_count - shift_rows, row_count, 1
    )
    mixed_in = (settled.astype(jnp.float32) + position_term).astype(jnp.bfloat16)
    block_out = jnp.dot(
        mixed_in.reshape(frame_count * row_count * col_count, channels),
        out_weight,
        preferred_element_type=jnp.float32,
    )
    return block_out.astype(jnp.bfloat16).reshape(
        frame_count, row_count, col_count, out_weight.shape[1]
    )


def solution(mesh):
    in_specs = (
        P("tm", "height", None, None),
        P("tm", "height", None, None),
        P("tm", "height", None, None),
        P(),
        P(),
        P(),
    )
    out_specs = P("tm", "height", None, None)
    return jax.shard_map(body, mesh=mesh, in_specs=in_specs, out_specs=out_specs, check_vma=False)
```

profile of v0, /device:TPU:1, one launch (start us, length us, event | category | flops | bytes accessed | tf_op | source)
XLA Modules:
  0.0 217.1 jit_solution(4091657852167401772)
XLA Ops:
  0.0 5.1 %pad_maximum_fusion = bf16[3,2,16,16,1536]{4,3,2,1,0:T(8,128)(2,1)} fusion(bf16[1,2,16,16,1536]{4,3,2,1,0:T(8,128)(2,1)} %bitcast.37, bf16[1,2,16,16,1536]{4,3,2,1,0:T(8,128)(2,1)} %bitcast.44, bf16[1,2,16,16,1536]{4,3,2,1,0:T(8,128)(2,1)} %bitcast.42), kind=kLoop, calls=%fused_computation.23 | loop fusion | flops 4718592 | bytes 9437184 | tf_op jit(solution)/shard_map/stack | solution.py:101
  5.1 3.2 %collective-permute-start = (bf16[3,2,16,16,1536]{4,3,2,1,0:T(8,128)(2,1)}, bf16[3,2,16,16,1536]{4,3,2,1,0:T(8,128)(2,1)}, u32[]{:S(2)}, u32[]{:S(2)}) collective-permute-start(bf16[3,2,16,16,1536]{4,3,2,1,0:T(8,128)(2,1)} %pad_maximum_fusion), channel_id=1, source_target_pairs={{0,3},{1,0},{2,1},{3,2},{4,7},{5,4},{6,5},{7,6},{8,11},{9,8},{10,9... | collective-permute-start | bytes 14155784 | tf_op jit(solution)/shard_map/ppermute | solution.py:14
  12.3 47.6 %collective-permute-done = bf16[3,2,16,16,1536]{4,3,2,1,0:T(8,128)(2,1)} collective-permute-done((bf16[3,2,16,16,1536]{4,3,2,1,0:T(8,128)(2,1)}, bf16[3,2,16,16,1536]{4,3,2,1,0:T(8,128)(2,1)}, u32[]{:S(2)}, u32[]{:S(2)}) %collective-permute-start) | collective-permute-done | bytes 4718624 | tf_op jit(solution)/shard_map/ppermute | solution.py:14
  59.9 3.7 %fusion.10 = bf16[3,2,16,16,1536]{4,3,2,1,0:T(8,128)(2,1)S(1)} fusion(s32[]{:T(128)S(6)} %select_n.29, bf16[1,2,16,16,1536]{4,3,2,1,0:T(8,128)(2,1)S(1)} %bitcast.43, bf16[1,2,16,16,1536]{4,3,2,1,0:T(8,128)(2,1)} %bitcast.45, bf16[1,2,16,16,1536]{4,3,2,1,0:T(8,128)(2,1)S(1)} %bitcast.38, bf16[3,2,16,16,1536]{4,3,2,1,0:T(8,128)(2,1)} %collective-permute-done), kind=kLoop, calls=%fused_computation.22 | loop fusion | flops 7077888 | bytes 14155780 | tf_op jit(solution)/shard_map/concatenate | solution.py:104
  63.6 3.7 %fusion.7 = bf16[3,2,16,16,1536]{4,3,2,1,0:T(8,128)(2,1)S(1)} fusion(s32[]{:T(128)S(6)} %select_n.31, bf16[3,2,16,16,1536]{4,3,2,1,0:T(8,128)(2,1)S(1)} %fusion.10), kind=kLoop, calls=%fused_computation.19 | loop fusion | flops 9437184 | bytes 9437188 | tf_op jit(solution)/shard_map/jit(_roll_dynamic)/concatenate | solution.py:106
  67.7 10.5 %collective-permute-start.1 = (bf16[3,16,16,1536]{3,2,1,0:T(8,128)(2,1)S(1)}, bf16[3,16,16,1536]{3,2,1,0:T(8,128)(2,1)S(1)}, u32[]{:S(2)}, u32[]{:S(2)}) collective-permute-start(bf16[3,16,16,1536]{3,2,1,0:T(8,128)(2,1)S(1)} %get-tuple-element.36), channel_id=1, source_target_pairs={{0,252},{4,0},{8,4},{12,8},{16,12},{20,16},{24,20},{28,24},{32,28}... | collective-permute-start | bytes 7077896 | tf_op jit(solution)/shard_map/ppermute | solution.py:14
  79.5 1.3 collective-permute-start.5
  80.8 4.9 %collective-permute-start.4 = (bf16[1,16,16,1536]{3,2,1,0:T(8,128)(2,1)}, bf16[1,16,16,1536]{3,2,1,0:T(8,128)(2,1)}, u32[]{:S(2)}, u32[]{:S(2)}) collective-permute-start(bf16[1,16,16,1536]{3,2,1,0:T(8,128)(2,1)} %get-tuple-element.42), channel_id=1, source_target_pairs={{0,4},{4,8},{8,12},{12,16},{16,20},{20,24},{24,28},{28,32},{32,36}... | collective-permute-start | bytes 2359304 | tf_op jit(solution)/shard_map/ppermute | solution.py:25
  85.7 43.5 %collective-permute-done.1 = bf16[3,16,16,1536]{3,2,1,0:T(8,128)(2,1)S(1)} collective-permute-done((bf16[3,16,16,1536]{3,2,1,0:T(8,128)(2,1)S(1)}, bf16[3,16,16,1536]{3,2,1,0:T(8,128)(2,1)S(1)}, u32[]{:S(2)}, u32[]{:S(2)}) %collective-permute-start.1) | collective-permute-done | bytes 2359328 | tf_op jit(solution)/shard_map/ppermute | solution.py:14
  129.7 1.6 copy.9
  131.3 1.6 copy.8
  132.9 1.6 copy.10
  134.5 4.9 %fusion.33 = (f32[2,2,12,128]{3,2,1,0:T(8,128)S(1)}, f32[2,2,12,128,128]{3,4,2,1,0:T(8,128)}) fusion(bf16[2,2,12,128,128]{4,3,2,1,0:T(8,128)(2,1)} %bitcast.50, bf16[2,2,12,128,128]{4,3,2,1,0:T(8,128)(2,1)} %bitcast.49), kind=kOutput, calls=%fused_computation.100 | convolution fusion | flops 203686016 | bytes 6316032 | tf_op jit(solution)/shard_map/sub | solution.py:36
  139.4 3.0 %convolution_convert_fusion.1 = bf16[2,2,12,128,128]{4,3,2,1,0:T(8,128)(2,1)S(1)} fusion(bf16[2,2,12,128,128]{4,3,2,1,0:T(8,128)(2,1)} %bitcast.51, f32[2,2,12,128,128]{3,4,2,1,0:T(8,128)} %get-tuple-element.46, f32[2,2,12,128]{3,2,1,0:T(8,128)S(1)} %get-tuple-element.45), kind=kOutput, calls=%fused_computation.46 | convolution fusion | flops 203685888 | bytes 6316032 | tf_op jit(solution)/shard_map/awhqk,awhkd->awhqd/dot_general | solution.py:78
  146.6 22.7 %collective-permute-done.2 = bf16[16,16,1536]{2,1,0:T(8,128)(2,1)} collective-permute-done((bf16[16,16,1536]{2,1,0:T(8,128)(2,1)}, bf16[16,16,1536]{2,1,0:T(8,128)(2,1)}, u32[]{:S(2)}, u32[]{:S(2)}) %collective-permute-start.2) | collective-permute-done | bytes 786464 | tf_op jit(solution)/shard_map/ppermute | solution.py:14
  169.3 2.4 %fusion.20 = bf16[2,16,16,1536]{3,2,1,0:T(8,128)(2,1)S(1)} fusion(s32[]{:T(128)S(6)} %select_n.33, bf16[1,16,16,1536]{3,2,1,0:T(8,128)(2,1)} %bitcast.19, bf16[1,16,16,1536]{3,2,1,0:T(8,128)(2,1)S(1)} %bitcast.46), kind=kLoop, calls=%fused_computation.53 | loop fusion | flops 6291456 | bytes 3145732 | tf_op jit(solution)/shard_map/jit(_roll_dynamic)/concatenate | solution.py:108
  173.2 1.9 collective-permute-start.6
  175.1 2.4 %collective-permute-start.7 = (bf16[4,1,16,1536]{3,2,1,0:T(8,128)(2,1)}, bf16[4,1,16,1536]{3,2,1,0:T(8,128)(2,1)S(1)}, u32[]{:S(2)}, u32[]{:S(2)}) collective-permute-start(bf16[4,1,16,1536]{3,2,1,0:T(8,128)(2,1)} %get-tuple-element.38), channel_id=1, source_target_pairs={{1,0},{2,1},{3,2},{5,4},{6,5},{7,6},{9,8},{10,9},{11,10},{13,12},{... | collective-permute-start | bytes 589832 | tf_op jit(solution)/shard_map/ppermute | solution.py:27
  177.5 1.9 slice_reduce_fusion.25
  180.7 1.9 slice_reduce_fusion.26
  182.7 9.3 %collective-permute-done.6 = bf16[4,1,16,1536]{3,2,1,0:T(8,128)(2,1)S(1)} collective-permute-done((bf16[4,1,16,1536]{3,2,1,0:T(8,128)(2,1)}, bf16[4,1,16,1536]{3,2,1,0:T(8,128)(2,1)S(1)}, u32[]{:S(2)}, u32[]{:S(2)}) %collective-permute-start.6) | collective-permute-done | bytes 196640 | tf_op jit(solution)/shard_map/ppermute | solution.py:25
  192.0 4.5 %fusion.6 = bf16[4,18,18,1536]{3,2,1,0:T(8,128)(2,1)S(1)} fusion(bf16[4,1,16,1536]{3,2,1,0:T(8,128)(2,1)S(1)} %collective-permute-done.7, bf16[4,16,16,1536]{3,2,1,0:T(8,128)(2,1)} %copy-done.1, bf16[4,1,16,1536]{3,2,1,0:T(8,128)(2,1)S(1)} %collective-permute-done.6), kind=kLoop, calls=%fused_computation.18 | loop fusion | flops 23887872 | bytes 7520256 | tf_op jit(solution)/shard_map/concatenate | solution.py:23
  196.6 14.1 %add_convert_fusion = bf16[2,16,16,1536]{3,2,1,0:T(8,128)(2,1)S(1)} fusion(bf16[2,16,16,1536]{3,2,1,0:T(8,128)(2,1)S(1)} %copy-done, bf16[4,16,16,1536]{3,2,1,0:T(8,128)(2,1)S(1)} %copy-done.2, s32[]{:T(128)S(6)} %select_n.34, bf16[2,16,16,1536]{3,2,1,0:T(8,128)(2,1)} %collective-permute-done.3, bf16[2,16,16,1536]{3,2,1,0:T(8,128)(2,1)S(1)} %fusion.20, ...), kind=kLoop, calls=%fused_computation.35 | loop fusion | flops 72351744 | bytes 39880708 | tf_op jit(solution)/shard_map/convert_element_type | solution.py:113
  210.7 6.4 %convolution_convert_fusion = bf16[512,3072]{1,0:T(8,128)(2,1)} fusion(bf16[512,1536]{1,0:T(8,128)(2,1)S(1)} %bitcast.48, bf16[1536,3072]{1,0:T(8,128)(2,1)S(1)} %bitcast.54), kind=kOutput, calls=%fused_computation.28 | convolution fusion | flops 4833411072 | bytes 14155776 | tf_op jit(solution)/shard_map/dot_general | solution.py:114
  (50 shorter events, 7.1 us)
Async XLA Ops:
  0.0 8.4 %copy-start.12 = (s32[2]{0:T(128)S(1)}, s32[2]{0:T(128)}, u32[]{:S(2)}) copy-start(s32[2]{0:T(128)} %param.9) | copy-start | bytes 28
  0.0 59.9 %copy-start = (bf16[2,16,16,1536]{3,2,1,0:T(8,128)(2,1)S(1)}, bf16[2,16,16,1536]{3,2,1,0:T(8,128)(2,1)}, u32[]{:S(2)}) copy-start(bf16[2,16,16,1536]{3,2,1,0:T(8,128)(2,1)} %param.8) | copy-start | bytes 4718596
  0.0 59.9 %copy-start.3 = (bf16[2,16,16,1536]{3,2,1,0:T(8,128)(2,1)S(1)}, bf16[2,16,16,1536]{3,2,1,0:T(8,128)(2,1)}, u32[]{:S(2)}) copy-start(bf16[2,16,16,1536]{3,2,1,0:T(8,128)(2,1)} %param.6) | copy-start | bytes 4718596
  5.1 54.7 %collective-permute-start = (bf16[3,2,16,16,1536]{4,3,2,1,0:T(8,128)(2,1)}, bf16[3,2,16,16,1536]{4,3,2,1,0:T(8,128)(2,1)}, u32[]{:S(2)}, u32[]{:S(2)}) collective-permute-start(bf16[3,2,16,16,1536]{4,3,2,1,0:T(8,128)(2,1)} %pad_maximum_fusion), channel_id=1, source_target_pairs={{0,3},{1,0},{2,1},{3,2},{4,7},{5,4},{6,5},{7,6},{8,11},{9,8},{10,9... | collective-permute-start | bytes 14155784 | tf_op jit(solution)/shard_map/ppermute | solution.py:14
  67.7 61.5 %collective-permute-start.1 = (bf16[3,16,16,1536]{3,2,1,0:T(8,128)(2,1)S(1)}, bf16[3,16,16,1536]{3,2,1,0:T(8,128)(2,1)S(1)}, u32[]{:S(2)}, u32[]{:S(2)}) collective-permute-start(bf16[3,16,16,1536]{3,2,1,0:T(8,128)(2,1)S(1)} %get-tuple-element.36), channel_id=1, source_target_pairs={{0,252},{4,0},{8,4},{12,8},{16,12},{20,16},{24,20},{28,24},{32,28}... | collective-permute-start | bytes 7077896 | tf_op jit(solution)/shard_map/ppermute | solution.py:14
  79.5 66.8 %collective-permute-start.5 = (bf16[1,16,16,1536]{3,2,1,0:T(8,128)(2,1)}, bf16[1,16,16,1536]{3,2,1,0:T(8,128)(2,1)S(1)}, u32[]{:S(2)}, u32[]{:S(2)}) collective-permute-start(bf16[1,16,16,1536]{3,2,1,0:T(8,128)(2,1)} %get-tuple-element.41), channel_id=1, source_target_pairs={{4,0},{8,4},{12,8},{16,12},{20,16},{24,20},{28,24},{32,28},{36,32}... | collective-permute-start | bytes 2359304 | tf_op jit(solution)/shard_map/ppermute | solution.py:27
  80.8 64.2 %collective-permute-start.4 = (bf16[1,16,16,1536]{3,2,1,0:T(8,128)(2,1)}, bf16[1,16,16,1536]{3,2,1,0:T(8,128)(2,1)}, u32[]{:S(2)}, u32[]{:S(2)}) collective-permute-start(bf16[1,16,16,1536]{3,2,1,0:T(8,128)(2,1)} %get-tuple-element.42), channel_id=1, source_target_pairs={{0,4},{4,8},{8,12},{12,16},{16,20},{20,24},{24,28},{28,32},{32,36}... | collective-permute-start | bytes 2359304 | tf_op jit(solution)/shard_map/ppermute | solution.py:25
  143.6 25.7 %collective-permute-start.2 = (bf16[16,16,1536]{2,1,0:T(8,128)(2,1)}, bf16[16,16,1536]{2,1,0:T(8,128)(2,1)}, u32[]{:S(2)}, u32[]{:S(2)}) collective-permute-start(bf16[16,16,1536]{2,1,0:T(8,128)(2,1)} %bitcast.18), channel_id=1, source_target_pairs={{0,4},{4,8},{8,12},{12,16},{16,20},{20,24},{24,28},{28,32},{32,36}... | collective-permute-start | bytes 2359304 | tf_op jit(solution)/shard_map/ppermute | solution.py:14
  146.3 23.0 %copy-start.4 = (bf16[1,16,16,1536]{3,2,1,0:T(8,128)(2,1)}, bf16[1,16,16,1536]{3,2,1,0:T(8,128)(2,1)S(1)}, u32[]{:S(2)}) copy-start(bf16[1,16,16,1536]{3,2,1,0:T(8,128)(2,1)S(1)} %collective-permute-done.5) | copy-start | bytes 2359300
  146.4 26.0 %copy-start.1 = (bf16[4,16,16,1536]{3,2,1,0:T(8,128)(2,1)}, bf16[4,16,16,1536]{3,2,1,0:T(8,128)(2,1)S(1)}, u32[]{:S(2)}) copy-start(bf16[4,16,16,1536]{3,2,1,0:T(8,128)(2,1)S(1)} %constant_dynamic-update-slice_fusion) | copy-start | bytes 9437188
  171.7 24.7 %collective-permute-start.3 = (bf16[2,16,16,1536]{3,2,1,0:T(8,128)(2,1)S(1)}, bf16[2,16,16,1536]{3,2,1,0:T(8,128)(2,1)}, u32[]{:S(2)}, u32[]{:S(2)}) collective-permute-start(bf16[2,16,16,1536]{3,2,1,0:T(8,128)(2,1)S(1)} %fusion.20), channel_id=1, source_target_pairs={{0,1},{1,2},{2,3},{3,0},{4,5},{5,6},{6,7},{7,4},{8,9},{9,10},{10,1... | collective-permute-start | bytes 4718600 | tf_op jit(solution)/shard_map/ppermute | solution.py:14
  173.2 18.8 %collective-permute-start.6 = (bf16[4,1,16,1536]{3,2,1,0:T(8,128)(2,1)}, bf16[4,1,16,1536]{3,2,1,0:T(8,128)(2,1)S(1)}, u32[]{:S(2)}, u32[]{:S(2)}) collective-permute-start(bf16[4,1,16,1536]{3,2,1,0:T(8,128)(2,1)} %get-tuple-element.37), channel_id=1, source_target_pairs={{0,1},{1,2},{2,3},{4,5},{5,6},{6,7},{8,9},{9,10},{10,11},{12,13},{... | collective-permute-start | bytes 589832 | tf_op jit(solution)/shard_map/ppermute | solution.py:25
  175.1 16.9 %collective-permute-start.7 = (bf16[4,1,16,1536]{3,2,1,0:T(8,128)(2,1)}, bf16[4,1,16,1536]{3,2,1,0:T(8,128)(2,1)S(1)}, u32[]{:S(2)}, u32[]{:S(2)}) collective-permute-start(bf16[4,1,16,1536]{3,2,1,0:T(8,128)(2,1)} %get-tuple-element.38), channel_id=1, source_target_pairs={{1,0},{2,1},{3,2},{5,4},{6,5},{7,6},{9,8},{10,9},{11,10},{13,12},{... | collective-permute-start | bytes 589832 | tf_op jit(solution)/shard_map/ppermute | solution.py:27
  182.6 13.9 %copy-start.2 = (bf16[4,16,16,1536]{3,2,1,0:T(8,128)(2,1)S(1)}, bf16[4,16,16,1536]{3,2,1,0:T(8,128)(2,1)}, u32[]{:S(2)}) copy-start(bf16[4,16,16,1536]{3,2,1,0:T(8,128)(2,1)} %copy-done.1) | copy-start | bytes 9437188
  182.6 13.9 %copy-start.5 = (bf16[1,16,16,1536]{3,2,1,0:T(8,128)(2,1)S(1)}, bf16[1,16,16,1536]{3,2,1,0:T(8,128)(2,1)}, u32[]{:S(2)}) copy-start(bf16[1,16,16,1536]{3,2,1,0:T(8,128)(2,1)} %copy-done.4) | copy-start | bytes 2359300
  182.6 13.9 %copy-start.6 = (f32[1536]{0:T(1024)S(1)}, f32[1536]{0:T(1024)}, u32[]{:S(2)}) copy-start(f32[1536]{0:T(1024)} %get-tuple-element.26) | copy-start | bytes 18436
  182.6 13.9 %copy-start.7 = (f32[1536]{0:T(1024)S(1)}, f32[1536]{0:T(1024)}, u32[]{:S(2)}) copy-start(f32[1536]{0:T(1024)} %get-tuple-element.27) | copy-start | bytes 18436
  182.7 13.9 %copy-start.8 = (f32[1536]{0:T(1024)S(1)}, f32[1536]{0:T(1024)}, u32[]{:S(2)}) copy-start(f32[1536]{0:T(1024)} %get-tuple-element.28) | copy-start | bytes 18436
  182.7 13.9 %copy-start.9 = (f32[1536]{0:T(1024)S(1)}, f32[1536]{0:T(1024)}, u32[]{:S(2)}) copy-start(f32[1536]{0:T(1024)} %get-tuple-element.29) | copy-start | bytes 18436
  182.7 13.9 %copy-start.10 = (f32[1536]{0:T(1024)S(1)}, f32[1536]{0:T(1024)}, u32[]{:S(2)}) copy-start(f32[1536]{0:T(1024)} %get-tuple-element.30) | copy-start | bytes 18436
  182.7 13.9 %copy-start.11 = (f32[1536]{0:T(1024)S(1)}, f32[1536]{0:T(1024)}, u32[]{:S(2)}) copy-start(f32[1536]{0:T(1024)} %get-tuple-element.31) | copy-start | bytes 18436
  192.0 18.7 %slice-start = ((s8[9437184]{0:T(1024)(128)(4,1)}), s8[4194304]{0:T(1024)(128)(4,1)S(1)}, s32[]{:S(2)}) async-start(s8[9437184]{0:T(1024)(128)(4,1)} %bitcast.53), calls=%async_computation | async-start | bytes 8388608
  196.5 14.2 %slice-start.1 = ((s8[9437184]{0:T(1024)(128)(4,1)}), s8[4194304]{0:T(1024)(128)(4,1)S(1)}, s32[]{:S(2)}) async-start(s8[9437184]{0:T(1024)(128)(4,1)} %bitcast.53), calls=%async_computation.1 | async-start | bytes 8388608
  196.6 14.2 %slice-start.2 = ((s8[9437184]{0:T(1024)(128)(4,1)}), s8[1048576]{0:T(1024)(128)(4,1)S(1)}, s32[]{:S(2)}) async-start(s8[9437184]{0:T(1024)(128)(4,1)} %bitcast.53), calls=%async_computation.2 | async-start | bytes 2097152
where the time goes:
time: 218 us; the launch traced here: 217 us
  waiting for transfers between devices  123 us (56%)
  other arithmetic  34 us (16%)
  starting transfers between devices  24.9 us (11%)
  local copies, waits for them, and re-layouts  14.6 us (7%)
  matrix products  14.3 us (7%)
  between operations  6.24 us (3%)
    ppermute x4, waiting for transfers between devices, shifted(): return lax.ppermute(value, axis, pairs)  114 us
    ppermute x4, starting transfers between devices, shifted(): return lax.ppermute(value, axis, pairs)  14.4 us
    convert_element_type x1, other arithmetic, body(): (settled.astype(jnp.float32) + position_term).astype(jnp.bfloat16)  14.1 us
    ppermute x2, waiting for transfers between devices, with_halo(): lax.ppermute(tail, axis, [(i, (i + 1) % count) for i in range(ends)])  9.26 us
    ppermute x2, starting transfers between devices, with_halo(): lax.ppermute(tail, axis, [(i, (i + 1) % count) for i in range(ends)])  6.81 us
    dot_general x1, matrix products, body(): jnp.dot(mixed_in.reshape(frame_count * row_count * col_count, channels),...  6.39 us
    another operation x1, other arithmetic, body(): stacked = jnp.stack([query_states, key_states, value_states])  5.14 us
    sub x1, matrix products, soft_weights(): spread = jnp.exp(scores - row_max)  4.89 us
  transfers between devices with their start and end apart: 8, of which 4 were waited for; matrix products, arithmetic and copies ran while one was open for 12% of the time, Pallas kernels for 0%

commit v1 on v0

v1 whole, which is shorter than its diff:
```python
import functools
import math

import jax
import jax.numpy as jnp
from jax import lax
from jax.experimental import pallas as pl
from jax.experimental.pallas import tpu as pltpu
from jax.sharding import PartitionSpec as P

HEAD_DIM = 128
MESH = pl.DeviceIdType.MESH
NEG = -1e30
SCALE = math.log2(math.e) / math.sqrt(HEAD_DIM)


def kernel(
    nt, heads_per, chunks, tile,
    shifts, q_hbm, k_hbm, v_hbm, cw, w_hbm, out_hbm,
    q, kv, hb, asm, mo, w, acc, mixed, ostage, ob, vext, colbias, same,
    lsem, zs, zr, asend, arecv, ms, mr, fs, fr, hs, hr, osem,
):
    lanes_per = heads_per * HEAD_DIM
    t = lax.axis_index("tm")
    h = lax.axis_index("height")
    core = lax.rem(h, 2)
    nxt = (lax.rem(t + 1, nt), h)
    prv = (lax.rem(t + nt - 1, nt), h)
    buddy = (t, h + 1 - 2 * core)
    across = (t, lax.rem(h + 2, 4))
    m_rows = pl.ds(8 * core, 8)
    h_rows = pl.ds(8 - 8 * core, 8)
    s_row = shifts[0]
    s_col = shifts[1]

    def lanes_of(g):
        return pl.ds(pl.multiple_of(g * lanes_per, 128), lanes_per)

    def remote(src, dst, ssem, rsem, dev):
        return pltpu.make_async_remote_copy(
            src_ref=src, dst_ref=dst, send_sem=ssem, recv_sem=rsem, device_id=dev, device_id_type=MESH
        )

    loads = [
        pltpu.make_async_copy(k_hbm, kv.at[0, 1:3], lsem.at[0]),
        pltpu.make_async_copy(v_hbm, kv.at[1, 1:3], lsem.at[1]),
        pltpu.make_async_copy(q_hbm, q, lsem.at[2]),
        pltpu.make_async_copy(w_hbm, w, lsem.at[3]),
    ]
    for load in loads:
        load.start()

    bar = pltpu.get_barrier_semaphore()
    for dev in (nxt, prv, buddy, across):
        pl.semaphore_signal(bar, inc=1, device_id=dev, device_id_type=MESH)
    pl.semaphore_wait(bar, 4)

    part_frames = (pl.ds(1, 2), pl.ds(0, 1), pl.ds(3, 1))

    def z_copy(phase, way, tensor, g):
        rows = (m_rows, h_rows)[phase]
        src = (k_hbm, v_hbm)[tensor].at[1 - way, rows, :, lanes_of(g)]
        dst = kv.at[tensor, 3 * way, rows, :, lanes_of(g)]
        return remote(src, dst, zs.at[phase, way, tensor, g], zr.at[phase, way, tensor, g], (nxt, prv)[way])

    def asm_copy(part, g):
        fr_ = part_frames[part]
        return remote(
            kv.at[1 - core, fr_, m_rows, :, lanes_of(g)], asm.at[fr_, :, :, lanes_of(g)],
            asend.at[part, g], arecv.at[part, g], buddy,
        )

    def x_copy(part, g):
        fr_ = part_frames[part]
        return remote(
            mo.at[fr_, :, :, lanes_of(g)], hb.at[core, fr_, 0:8, :, lanes_of(g)],
            ms.at[part, g], mr.at[part, g], across,
        )

    def fwd_copy(part, g):
        fr_ = part_frames[part]
        return remote(
            hb.at[core, fr_, 0:8, :, lanes_of(g)], hb.at[core, fr_, 0:8, :, lanes_of(g)],
            fs.at[part, g], fr.at[part, g], buddy,
        )

    def halo_copy(part, g):
        fr_ = part_frames[part]
        return remote(
            kv.at[:, fr_, h_rows, :, lanes_of(g)], hb.at[:, fr_, 8:16, :, lanes_of(g)],
            hs.at[part, g], hr.at[part, g], buddy,
        )

    def assemble(part, g):
        for frame in ((1, 2), (0,), (3,))[part]:
            for j in range(8):
                ours = (s_row <= j).astype(jnp.int32) == core
                mine = kv[core, frame, 8 * core + j, :, lanes_of(g)]
                mo[frame, j, :, lanes_of(g)] = jnp.where(ours, mine, asm[frame, j, :, lanes_of(g)])

    loads[0].wait()
    loads[1].wait()

    @pl.loop(0, chunks)
    def _(g):
        asm_copy(0, g).start()

    for phase in range(2):
        @pl.loop(0, chunks)
        def _(g):
            for way in range(2):
                for tensor in range(2):
                    z_copy(phase, way, tensor, g).start()

    @pl.loop(0, chunks)
    def _(g):
        halo_copy(0, g).start()

    qi = lax.broadcasted_iota(jnp.int32, (128, 256), 0)
    ki = lax.broadcasted_iota(jnp.int32, (128, 256), 1)
    q_win = ((qi % 16 - s_col + 16) % 16) // 8
    k_win = ((ki % 16 - s_col + 16) % 16) // 8
    colbias[...] = jnp.where(q_win == k_win, 0.0, NEG)
    q_low = (qi // 16 >= s_row).astype(jnp.int32)
    k_low = (ki % 128 // 16 >= s_row).astype(jnp.int32)
    same[...] = (q_low == k_low).astype(jnp.float32)

    @pl.loop(0, chunks)
    def _(g):
        asm_copy(0, g).wait_recv()
        assemble(0, g)
        x_copy(0, g).start()

    def corner_send(g):
        for part in (1, 2):
            asm_copy(part, g).wait_recv()
            assemble(part, g)
            x_copy(part, g).start()

    @pl.loop(0, chunks + 1)
    def _(g):
        @pl.when(g < chunks)
        def _():
            for way in range(2):
                for tensor in range(2):
                    z_copy(0, way, tensor, g).wait_recv()
            for part in (1, 2):
                asm_copy(part, g).start()
            x_copy(0, g).wait_recv()
            fwd_copy(0, g).start()

        @pl.when(g > 0)
        def _():
            corner_send(g - 1)

    loads[2].wait()
    loads[3].wait()

    low = [s_row <= j for j in range(8)]

    def slots(ref, lead, picks, lanes):
        return [
            jnp.where(pick, ref[(*lead, j, slice(None), lanes)], ref[(*lead, 8 + j, slice(None), lanes)])
            for j, pick in enumerate(picks)
        ]

    r_one = low
    r_two = [s_row > j for j in range(8)]
    r_halo = [(s_row <= j).astype(jnp.int32) != core for j in range(8)]

    def weights_of(scores):
        z = scores * SCALE + colbias[...]
        e = jnp.exp2(z - jnp.max(z, axis=1, keepdims=True))
        return e, 1.0 / jnp.sum(e, axis=1, keepdims=True)

    def dot_t(a, b):
        return lax.dot_general(a, b, (((1,), (1,)), ((), ())), preferred_element_type=jnp.float32)

    def dot(a, b):
        return jnp.dot(a, b, preferred_element_type=jnp.float32)

    def attend(frame, lanes):
        frames = (0, 1) if frame == 0 else (2, 3)

        def keys(ref, tensor, rows):
            return jnp.concatenate([x for f in frames for x in slots(ref, (tensor, f), rows, lanes)], axis=0)

        q_one = jnp.concatenate(slots(q, (frame,), r_one, lanes), axis=0)
        e, inv = weights_of(dot_t(q_one, keys(kv, 0, r_one)))
        one = (dot(e.astype(jnp.bfloat16), keys(kv, 1, r_one)) * inv).astype(jnp.bfloat16)

        q_two = jnp.concatenate(slots(q, (frame,), r_two, lanes), axis=0)
        pick = same[...] > 0.5
        e, inv = weights_of(
            jnp.where(pick, dot_t(q_two, keys(kv, 0, r_two)), dot_t(q_two, keys(hb, 0, r_halo)))
        )
        near = jnp.where(pick, e, 0.0).astype(jnp.bfloat16)
        far = jnp.where(pick, 0.0, e).astype(jnp.bfloat16)
        two = ((dot(near, keys(kv, 1, r_two)) + dot(far, keys(hb, 1, r_halo))) * inv).astype(jnp.bfloat16)
        for j in range(8):
            a = one[16 * j : 16 * j + 16]
            b = two[16 * j : 16 * j + 16]
            ob[frame, j] = jnp.where(low[j], a, b)
            ob[frame, 8 + j] = jnp.where(low[j], b, a)

    def convolve(lanes, mixed_lanes):
        keep_frame = (t > 0, None, None, t < nt - 1)
        for f in range(4):
            top = hb[1, f, 7 + 8 * core, :, lanes].astype(jnp.float32)
            bottom = hb[1, f, 8 - 8 * core, :, lanes].astype(jnp.float32)
            body = kv[1, f, :, :, lanes].astype(jnp.float32)
            top = jnp.where(h > 0, top, 0.0)
            bottom = jnp.where(h < 3, bottom, 0.0)
            if keep_frame[f] is not None:
                top = jnp.where(keep_frame[f], top, 0.0)
                bottom = jnp.where(keep_frame[f], bottom, 0.0)
                body = jnp.where(keep_frame[f], body, 0.0)
            vext[f, 0] = top
            vext[f, 17] = bottom
            vext[f, 1:17] = body
        col = lax.broadcasted_iota(jnp.int32, (4, 16, 128), 1)
        for f in range(2):
            @pl.loop(0, 4)
            def _(rb):
                sums = [jnp.zeros((4, 16, 128), jnp.float32) for _ in range(3)]
                for dt in range(3):
                    for dr in range(3):
                        slab = vext[f + dt, pl.ds(4 * rb + dr, 4)]
                        for dc in range(3):
                            tap = 9 * dt + 3 * dr + dc
                            sums[dc] = sums[dc] + cw[tap : tap + 1, lanes][None] * slab
                left = jnp.where(col > 0, pltpu.roll(sums[0], 1, 1), 0.0)
                right = jnp.where(col < 15, pltpu.roll(sums[2], 15, 1), 0.0)
                term = sums[1] + left + right
                win = ob[f, pl.ds(4 * rb, 4)].astype(jnp.float32)
                mixed[f, pl.ds(4 * rb, 4), :, mixed_lanes] = (win + term).astype(jnp.bfloat16)

    def out_copy(i):
        cols = pl.ds(pl.multiple_of(i * tile, tile), tile)
        return pltpu.make_async_copy(ostage.at[:, cols], out_hbm.at[:, cols], osem.at[i])

    tiles = acc.shape[1] // tile

    def project(g):
        left = mixed[...].reshape(512, lanes_per)

        @pl.loop(0, tiles)
        def _(i):
            cols = pl.ds(pl.multiple_of(i * tile, tile), tile)
            part = dot(left, w[pl.ds(pl.multiple_of(g * lanes_per, 128), lanes_per), cols])

            @pl.when(g == 0)
            def _():
                acc[:, cols] = part

            @pl.when((g > 0) & (g < chunks - 1))
            def _():
                acc[:, cols] = acc[:, cols] + part

            @pl.when(g == chunks - 1)
            def _():
                ostage[:, cols] = (acc[:, cols] + part).astype(jnp.bfloat16)
                out_copy(i).start()

    def compute(g):
        halo_copy(0, g).wait_recv()
        fwd_copy(0, g).wait_recv()
        for part in (1, 2):
            halo_copy(part, g).wait_recv()
            fwd_copy(part, g).wait_recv()

        @pl.loop(0, heads_per)
        def _(i):
            lanes = pl.ds(pl.multiple_of(g * lanes_per + i * 128, 128), 128)
            for frame in range(2):
                attend(frame, lanes)
            convolve(lanes, pl.ds(pl.multiple_of(i * 128, 128), 128))

        project(g)

    @pl.loop(0, chunks + 1)
    def _(g):
        @pl.when(g < chunks)
        def _():
            for way in range(2):
                for tensor in range(2):
                    z_copy(1, way, tensor, g).wait_recv()
            for part in (1, 2):
                halo_copy(part, g).start()
            for part in (1, 2):
                x_copy(part, g).wait_recv()
                fwd_copy(part, g).start()

        @pl.when(g > 0)
        def _():
            compute(g - 1)

    @pl.loop(0, chunks)
    def _(g):
        for phase in range(2):
            for way in range(2):
                for tensor in range(2):
                    z_copy(phase, way, tensor, g).wait_send()
        for part in range(3):
            asm_copy(part, g).wait_send()
            x_copy(part, g).wait_send()
            fwd_copy(part, g).wait_send()
            halo_copy(part, g).wait_send()

    @pl.loop(0, tiles)
    def _(i):
        out_copy(i).wait()


def body(nt, query_states, key_states, value_states, shifts, conv_kernel, out_weight):
    frames, rows, cols, channels = query_states.shape
    width = out_weight.shape[1]
    heads = channels // HEAD_DIM
    heads_per = 2 if heads % 2 == 0 and heads > 2 else 1
    chunks = heads // heads_per
    tile = 256
    any_spec = pl.BlockSpec(memory_space=pl.ANY)
    dma = pltpu.SemaphoreType.DMA
    bf16 = jnp.bfloat16
    out = pl.pallas_call(
        functools.partial(kernel, nt, heads_per, chunks, tile),
        out_shape=jax.ShapeDtypeStruct((frames * rows * cols, width), bf16),
        in_specs=[
            pl.BlockSpec(memory_space=pltpu.SMEM),
            any_spec, any_spec, any_spec,
            pl.BlockSpec(memory_space=pltpu.VMEM),
            any_spec,
        ],
        out_specs=any_spec,
        scratch_shapes=[
            pltpu.VMEM((2, 16, 16, channels), bf16),
            pltpu.VMEM((2, 4, 16, 16, channels), bf16),
            pltpu.VMEM((2, 4, 16, 16, channels), bf16),
            pltpu.VMEM((4, 8, 16, channels), bf16),
            pltpu.VMEM((4, 8, 16, channels), bf16),
            pltpu.VMEM((channels, width), bf16),
            pltpu.VMEM((512, width), jnp.float32),
            pltpu.VMEM((2, 16, 16, heads_per * HEAD_DIM), bf16),
            pltpu.VMEM((512, width), bf16),
            pltpu.VMEM((2, 16, 16, HEAD_DIM), bf16),
            pltpu.VMEM((4, 18, 16, HEAD_DIM), jnp.float32),
            pltpu.VMEM((128, 256), jnp.float32),
            pltpu.VMEM((128, 256), jnp.float32),
            dma((4,)),
            dma((2, 2, 2, chunks)), dma((2, 2, 2, chunks)),
            dma((3, chunks)), dma((3, chunks)),
            dma((3, chunks)), dma((3, chunks)),
            dma((3, chunks)), dma((3, chunks)),
            dma((3, chunks)), dma((3, chunks)),
            dma((width // tile,)),
        ],
        compiler_params=pltpu.CompilerParams(
            collective_id=0, has_side_effects=True, vmem_limit_bytes=60 * 2**20
        ),
        name="window_block",
    )(shifts, query_states, key_states, value_states, conv_kernel, out_weight)
    return out.reshape(frames, rows, cols, width)


def solution(mesh):
    in_specs = (
        P("tm", "height", None, None),
        P("tm", "height", None, None),
        P("tm", "height", None, None),
        P(),
        P(),
        P(),
    )
    out_specs = P("tm", "height", None, None)
    return jax.shard_map(
        functools.partial(body, mesh.shape["tm"]), mesh=mesh, in_specs=in_specs, out_specs=out_specs, check_vma=False
    )
```

time: 218 us -> 118 us (0.54)
  the two profiles are of different devices: /device:TPU:1 before, /device:TPU:25 now
where the time goes in v1:
time: 118 us
  Pallas kernels  114 us (97%)
  local copies, waits for them, and re-layouts  3.88 us (3%)
    pallas_call x1, Pallas kernels, body(): pl.pallas_call(functools.partial(kernel, nt, heads_per, chunks, tile), ou...  114 us
    unnamed x1, local copies, waits for them, and re-layouts  3.88 us

profile of v1, /device:TPU:25, one launch (start us, length us, event | category | flops | bytes accessed | tf_op | source)
XLA Modules:
  0.0 117.9 jit_solution(202382278171640698)
XLA Ops:
  0.0 114.0 %window_block.1 = bf16[512,3072]{1,0:T(8,128)(2,1)} custom-call(s32[2]{0:T(128)} %shifts.1, bf16[2,16,16,1536]{3,2,1,0:T(8,128)(2,1)} %q_hbm.1, bf16[2,16,16,1536]{3,2,1,0:T(8,128)(2,1)} %k_hbm.1, bf16[2,16,16,1536]{3,2,1,0:T(8,128)(2,1)} %v_hbm.1, f32[27,1536]{1,0:T(8,128)} %cw.1, bf16[1536,3072]{1,0:T(8,128)(2,1)} %w_hbm.1), custom_call_target="tpu_custom_call" | custom-call | tf_op jit(solution)/shard_map/window_block/pallas_call | solution.py:325
  114.0 3.9 %copy.8 = bf16[2,16,16,3072]{3,2,1,0:T(8,128)(2,1)} copy(bf16[2,16,16,3072]{3,2,1,0:T(8,128)(2,1)} %bitcast.1) | data formatting | bytes 6291456

commit v2 on v1

--- a/solution.py
+++ b/solution.py
@@ -15,12 +15,11 @@
 
 
 def kernel(
-    nt, heads_per, chunks, tile,
-    shifts, q_hbm, k_hbm, v_hbm, cw, w_hbm, out_hbm,
-    q, kv, hb, asm, mo, w, acc, mixed, ostage, ob, vext, colbias, same,
-    lsem, zs, zr, asend, arecv, ms, mr, fs, fr, hs, hr, osem,
+    nt, chunks, lag, lead, early, relayed,
+    shifts, q_hbm, k_hbm, v_hbm, cw, out_hbm,
+    q, kv, hb, asm, mo, mixed, ob, vext, colbias, same, rb,
+    lsem, zs, zr, asend, arecv, ms, mr, fs, fr, hs, hr, rs, rr, osem,
 ):
-    lanes_per = heads_per * HEAD_DIM
     t = lax.axis_index("tm")
     h = lax.axis_index("height")
     core = lax.rem(h, 2)
@@ -34,7 +33,7 @@
     s_col = shifts[1]
 
     def lanes_of(g):
-        return pl.ds(pl.multiple_of(g * lanes_per, 128), lanes_per)
+        return pl.ds(pl.multiple_of(g * HEAD_DIM, HEAD_DIM), HEAD_DIM)
 
     def remote(src, dst, ssem, rsem, dev):
         return pltpu.make_async_remote_copy(
@@ -45,15 +44,45 @@
         pltpu.make_async_copy(k_hbm, kv.at[0, 1:3], lsem.at[0]),
         pltpu.make_async_copy(v_hbm, kv.at[1, 1:3], lsem.at[1]),
         pltpu.make_async_copy(q_hbm, q, lsem.at[2]),
-        pltpu.make_async_copy(w_hbm, w, lsem.at[3]),
     ]
     for load in loads:
         load.start()
 
+    greet = [(None, dev) for dev in (nxt, prv, buddy, across)]
+    if relayed:
+        half, nz = nt // 2, nt // 8
+        base = t // half * half
+        other = half - base
+        y = t % half // nz
+        first, last = t % half == 0, t % half == half - 1
+        middle = (y == 1) | (y == 2)
+        relay_up = (t % nz == 0) & middle
+        relay_down = (t % nz == nz - 1) & middle
+        relay = relay_up | relay_down
+        slot_way = jnp.where(relay_up, 0, 1)
+        target = jnp.where(relay_up, other, other + half - 1)
+        for p in (1, 2):
+            greet.append((last, (base + nz * p, h)))
+            greet.append((first, (other + nz * p, h)))
+            greet.append((first, (base + nz * p + nz - 1, h)))
+            greet.append((last, (other + nz * p + nz - 1, h)))
+        greet.append((relay_up, (base + half - 1, h)))
+        greet.append((relay_up, (other, h)))
+        greet.append((relay_down, (base, h)))
+        greet.append((relay_down, (other + half - 1, h)))
+
     bar = pltpu.get_barrier_semaphore()
-    for dev in (nxt, prv, buddy, across):
-        pl.semaphore_signal(bar, inc=1, device_id=dev, device_id_type=MESH)
-    pl.semaphore_wait(bar, 4)
+    met = 0
+    for cond, dev in greet:
+        if cond is None:
+            pl.semaphore_signal(bar, inc=1, device_id=dev, device_id_type=MESH)
+            met = met + 1
+        else:
+            @pl.when(cond)
+            def _():
+                pl.semaphore_signal(bar, inc=1, device_id=dev, device_id_type=MESH)
+            met = met + jnp.where(cond, 1, 0)
+    pl.semaphore_wait(bar, met)
 
     part_frames = (pl.ds(1, 2), pl.ds(0, 1), pl.ds(3, 1))
 
@@ -62,6 +91,45 @@
         src = (k_hbm, v_hbm)[tensor].at[1 - way, rows, :, lanes_of(g)]
         dst = kv.at[tensor, 3 * way, rows, :, lanes_of(g)]
         return remote(src, dst, zs.at[phase, way, tensor, g], zr.at[phase, way, tensor, g], (nxt, prv)[way])
+
+    def z_start(phase, way, tensor, g):
+        if not relayed:
+            z_copy(phase, way, tensor, g).start()
+            return
+        p = g % 3
+        detour = (last, first)[way] & (p > 0)
+
+        @pl.when(detour)
+        def _():
+            rows = (m_rows, h_rows)[phase]
+            src = (k_hbm, v_hbm)[tensor].at[1 - way, rows, :, lanes_of(g)]
+            remote(
+                src, rb.at[g // 3, phase, tensor], zs.at[phase, way, tensor, g], rr.at[g // 3, phase, tensor],
+                (base + nz * p + (0, nz - 1)[way], h),
+            ).start()
+
+        @pl.when(jnp.logical_not(detour))
+        def _():
+            z_copy(phase, way, tensor, g).start()
+
+    def relay_copy(phase, tensor, g):
+        rows = (m_rows, h_rows)[phase]
+        return remote(
+            rb.at[g // 3, phase, tensor], kv.at[tensor, 3 * slot_way, rows, :, lanes_of(g)],
+            rs.at[g // 3, phase, tensor], zr.at[phase, slot_way, tensor, g], (target, h),
+        )
+
+    def relay_incoming(phase, tensor, g):
+        slot = rb.at[g // 3, phase, tensor]
+        return remote(slot, slot, rs.at[g // 3, phase, tensor], rr.at[g // 3, phase, tensor], (target, h))
+
+    def relay_step(phase, g):
+        if relayed:
+            @pl.when(relay & (g % 3 == y))
+            def _():
+                for tensor in range(2):
+                    relay_incoming(phase, tensor, g).wait_recv()
+                    relay_copy(phase, tensor, g).start()
 
     def asm_copy(part, g):
         fr_ = part_frames[part]
@@ -105,12 +173,19 @@
     def _(g):
         asm_copy(0, g).start()
 
-    for phase in range(2):
-        @pl.loop(0, chunks)
-        def _(g):
+    @pl.loop(0, chunks + lag)
+    def _(i):
+        @pl.when(i < chunks)
+        def _():
             for way in range(2):
                 for tensor in range(2):
-                    z_copy(phase, way, tensor, g).start()
+                    z_start(0, way, tensor, i)
+
+        @pl.when(i >= lag)
+        def _():
+            for way in range(2):
+                for tensor in range(2):
+                    z_start(1, way, tensor, i - lag)
 
     @pl.loop(0, chunks)
     def _(g):
@@ -125,36 +200,16 @@
     k_low = (ki % 128 // 16 >= s_row).astype(jnp.int32)
     same[...] = (q_low == k_low).astype(jnp.float32)
 
-    @pl.loop(0, chunks)
+    def pack_and_send(part, g):
+        asm_copy(part, g).wait_recv()
+        assemble(part, g)
+        x_copy(part, g).start()
+
+    @pl.loop(0, lead)
     def _(g):
-        asm_copy(0, g).wait_recv()
-        assemble(0, g)
-        x_copy(0, g).start()
-
-    def corner_send(g):
-        for part in (1, 2):
-            asm_copy(part, g).wait_recv()
-            assemble(part, g)
-            x_copy(part, g).start()
-
-    @pl.loop(0, chunks + 1)
-    def _(g):
-        @pl.when(g < chunks)
-        def _():
-            for way in range(2):
-                for tensor in range(2):
-                    z_copy(0, way, tensor, g).wait_recv()
-            for part in (1, 2):
-                asm_copy(part, g).start()
-            x_copy(0, g).wait_recv()
-            fwd_copy(0, g).start()
-
-        @pl.when(g > 0)
-        def _():
-            corner_send(g - 1)
+        pack_and_send(0, g)
 
     loads[2].wait()
-    loads[3].wait()
 
     low = [s_row <= j for j in range(8)]
 
@@ -235,65 +290,73 @@
                 win = ob[f, pl.ds(4 * rb, 4)].astype(jnp.float32)
                 mixed[f, pl.ds(4 * rb, 4), :, mixed_lanes] = (win + term).astype(jnp.bfloat16)
 
-    def out_copy(i):
-        cols = pl.ds(pl.multiple_of(i * tile, tile), tile)
-        return pltpu.make_async_copy(ostage.at[:, cols], out_hbm.at[:, cols], osem.at[i])
-
-    tiles = acc.shape[1] // tile
-
-    def project(g):
-        left = mixed[...].reshape(512, lanes_per)
-
-        @pl.loop(0, tiles)
-        def _(i):
-            cols = pl.ds(pl.multiple_of(i * tile, tile), tile)
-            part = dot(left, w[pl.ds(pl.multiple_of(g * lanes_per, 128), lanes_per), cols])
-
-            @pl.when(g == 0)
-            def _():
-                acc[:, cols] = part
-
-            @pl.when((g > 0) & (g < chunks - 1))
-            def _():
-                acc[:, cols] = acc[:, cols] + part
-
-            @pl.when(g == chunks - 1)
-            def _():
-                ostage[:, cols] = (acc[:, cols] + part).astype(jnp.bfloat16)
-                out_copy(i).start()
-
-    def compute(g):
-        halo_copy(0, g).wait_recv()
-        fwd_copy(0, g).wait_recv()
-        for part in (1, 2):
-            halo_copy(part, g).wait_recv()
-            fwd_copy(part, g).wait_recv()
-
-        @pl.loop(0, heads_per)
-        def _(i):
-            lanes = pl.ds(pl.multiple_of(g * lanes_per + i * 128, 128), 128)
-            for frame in range(2):
-                attend(frame, lanes)
-            convolve(lanes, pl.ds(pl.multiple_of(i * 128, 128), 128))
-
-        project(g)
-
-    @pl.loop(0, chunks + 1)
-    def _(g):
-        @pl.when(g < chunks)
-        def _():
+    def out_copy(g):
+        return pltpu.make_async_copy(mixed.at[:, :, :, lanes_of(g)], out_hbm.at[:, :, :, lanes_of(g)], osem.at[g])
+
+    for i in range(early):
+        relay_step(0, i)
+        if i >= lag:
+            relay_step(1, i - lag)
+
+    @pl.loop(0, chunks + 3)
+    def _(i):
+        @pl.when(i + early < chunks)
+        def _():
+            relay_step(0, i + early)
+
+        @pl.when((i + early >= lag) & (i + early < chunks + lag))
+        def _():
+            relay_step(1, i + early - lag)
+
+        @pl.when(i < chunks)
+        def _():
+            for way in range(2):
+                for tensor in range(2):
+                    z_copy(0, way, tensor, i).wait_recv()
+            for part in (1, 2):
+                asm_copy(part, i).start()
+
+        @pl.when((i >= 2) & (i < chunks + 2))
+        def _():
+            g = i - 2
+            x_copy(0, g).wait_recv()
+            fwd_copy(0, g).start()
+
+        @pl.when((i >= 1) & (i < chunks + 1))
+        def _():
+            for part in (1, 2):
+                pack_and_send(part, i - 1)
+
+        @pl.when(i + lead < chunks)
+        def _():
+            pack_and_send(0, i + lead)
+
+        @pl.when((i >= 2) & (i < chunks + 2))
+        def _():
+            g = i - 2
             for way in range(2):
                 for tensor in range(2):
                     z_copy(1, way, tensor, g).wait_recv()
             for part in (1, 2):
                 halo_copy(part, g).start()
+
+        @pl.when((i >= 2) & (i < chunks + 2))
+        def _():
+            g = i - 2
             for part in (1, 2):
                 x_copy(part, g).wait_recv()
                 fwd_copy(part, g).start()
 
-        @pl.when(g > 0)
-        def _():
-            compute(g - 1)
+        @pl.when(i >= 3)
+        def _():
+            g = i - 3
+            for part in range(3):
+                halo_copy(part, g).wait_recv()
+                fwd_copy(part, g).wait_recv()
+            for frame in range(2):
+                attend(frame, lanes_of(g))
+            convolve(lanes_of(g), lanes_of(g))
+            out_copy(g).start()
 
     @pl.loop(0, chunks)
     def _(g):
@@ -301,35 +364,37 @@
             for way in range(2):
                 for tensor in range(2):
                     z_copy(phase, way, tensor, g).wait_send()
+            if relayed:
+                @pl.when(relay & (g % 3 == y))
+                def _():
+                    for tensor in range(2):
+                        relay_copy(phase, tensor, g).wait_send()
         for part in range(3):
             asm_copy(part, g).wait_send()
             x_copy(part, g).wait_send()
             fwd_copy(part, g).wait_send()
             halo_copy(part, g).wait_send()
-
-    @pl.loop(0, tiles)
-    def _(i):
-        out_copy(i).wait()
+        out_copy(g).wait()
 
 
 def body(nt, query_states, key_states, value_states, shifts, conv_kernel, out_weight):
     frames, rows, cols, channels = query_states.shape
     width = out_weight.shape[1]
     heads = channels // HEAD_DIM
-    heads_per = 2 if heads % 2 == 0 and heads > 2 else 1
-    chunks = heads // heads_per
-    tile = 256
+    lag = 2
+    early = 2
+    lead = min(4, heads)
+    relayed = nt == 64 and heads % 3 == 0
     any_spec = pl.BlockSpec(memory_space=pl.ANY)
     dma = pltpu.SemaphoreType.DMA
     bf16 = jnp.bfloat16
-    out = pl.pallas_call(
-        functools.partial(kernel, nt, heads_per, chunks, tile),
-        out_shape=jax.ShapeDtypeStruct((frames * rows * cols, width), bf16),
+    mixed = pl.pallas_call(
+        functools.partial(kernel, nt, heads, lag, lead, early, relayed),
+        out_shape=jax.ShapeDtypeStruct((frames, rows, cols, channels), bf16),
         in_specs=[
             pl.BlockSpec(memory_space=pltpu.SMEM),
             any_spec, any_spec, any_spec,
             pl.BlockSpec(memory_space=pltpu.VMEM),
-            any_spec,
         ],
         out_specs=any_spec,
         scratch_shapes=[
@@ -338,28 +403,30 @@
             pltpu.VMEM((2, 4, 16, 16, channels), bf16),
             pltpu.VMEM((4, 8, 16, channels), bf16),
             pltpu.VMEM((4, 8, 16, channels), bf16),
-            pltpu.VMEM((channels, width), bf16),
-            pltpu.VMEM((512, width), jnp.float32),
-            pltpu.VMEM((2, 16, 16, heads_per * HEAD_DIM), bf16),
-            pltpu.VMEM((512, width), bf16),
+            pltpu.VMEM((2, 16, 16, channels), bf16),
             pltpu.VMEM((2, 16, 16, HEAD_DIM), bf16),
             pltpu.VMEM((4, 18, 16, HEAD_DIM), jnp.float32),
             pltpu.VMEM((128, 256), jnp.float32),
             pltpu.VMEM((128, 256), jnp.float32),
-            dma((4,)),
-            dma((2, 2, 2, chunks)), dma((2, 2, 2, chunks)),
-            dma((3, chunks)), dma((3, chunks)),
-            dma((3, chunks)), dma((3, chunks)),
-            dma((3, chunks)), dma((3, chunks)),
-            dma((3, chunks)), dma((3, chunks)),
-            dma((width // tile,)),
+            pltpu.VMEM((max(1, heads // 3), 2, 2, 8, 16, HEAD_DIM), bf16),
+            dma((3,)),
+            dma((2, 2, 2, heads)), dma((2, 2, 2, heads)),
+            dma((3, heads)), dma((3, heads)),
+            dma((3, heads)), dma((3, heads)),
+            dma((3, heads)), dma((3, heads)),
+            dma((3, heads)), dma((3, heads)),
+            dma((max(1, heads // 3), 2, 2)), dma((max(1, heads // 3), 2, 2)),
+            dma((heads,)),
         ],
         compiler_params=pltpu.CompilerParams(
             collective_id=0, has_side_effects=True, vmem_limit_bytes=60 * 2**20
         ),
         name="window_block",
-    )(shifts, query_states, key_states, value_states, conv_kernel, out_weight)
-    return out.reshape(frames, rows, cols, width)
+    )(shifts, query_states, key_states, value_states, conv_kernel)
+    block_out = jnp.dot(
+        mixed.reshape(frames * rows * cols, channels), out_weight, preferred_element_type=jnp.float32
+    )
+    return block_out.astype(bf16).reshape(frames, rows, cols, width)
 
 
 def solution(mesh):

time: 118 us -> 82.4 us (0.70)
  the two profiles are of different devices: /device:TPU:25 before, /device:TPU:1 now
where the time goes in v2:
time: 82.4 us; the launch traced here: 81.2 us
  Pallas kernels  71.9 us (87%)
  matrix products  9.22 us (11%)
    pallas_call x1, Pallas kernels, body(): pl.pallas_call(functools.partial(kernel, nt, heads, lag, lead, early, rel...  71.9 us
    dot_general x1, matrix products, body(): jnp.dot(mixed.reshape(frames * rows * cols, channels), out_weight, prefer...  9.22 us

profile of v2, /device:TPU:1, one launch (start us, length us, event | category | flops | bytes accessed | tf_op | source)
XLA Modules:
  0.0 81.2 jit_solution(2300079534711906871)
XLA Ops:
  0.0 71.9 %window_block.1 = bf16[2,16,16,1536]{3,2,1,0:T(8,128)(2,1)} custom-call(s32[2]{0:T(128)} %shifts.1, bf16[2,16,16,1536]{3,2,1,0:T(8,128)(2,1)} %q_hbm.1, bf16[2,16,16,1536]{3,2,1,0:T(8,128)(2,1)} %k_hbm.1, bf16[2,16,16,1536]{3,2,1,0:T(8,128)(2,1)} %v_hbm.1, f32[27,1536]{1,0:T(8,128)} %cw.1), custom_call_target="tpu_custom_call" | custom-call | tf_op jit(solution)/shard_map/window_block/pallas_call | solution.py:391
  71.9 9.2 %convolution_convert_fusion = bf16[512,3072]{1,0:T(8,128)(2,1)} fusion(bf16[512,1536]{1,0:T(8,128)(2,1)} %bitcast.4, bf16[1536,3072]{1,0:T(8,128)(2,1)} %param.11), kind=kOutput, calls=%fused_computation | convolution fusion | flops 4833411072 | bytes 14155776 | tf_op jit(solution)/shard_map/dot_general | solution.py:426

commit v3 on v2

--- a/solution.py
+++ b/solution.py
@@ -11,14 +11,16 @@
 HEAD_DIM = 128
 MESH = pl.DeviceIdType.MESH
 NEG = -1e30
+GROUP = 4 * HEAD_DIM
+TILE = 512
 SCALE = math.log2(math.e) / math.sqrt(HEAD_DIM)
 
 
 def kernel(
-    nt, chunks, lag, lead, early, relayed,
-    shifts, q_hbm, k_hbm, v_hbm, cw, out_hbm,
-    q, kv, hb, asm, mo, mixed, ob, vext, colbias, same, rb,
-    lsem, zs, zr, asend, arecv, ms, mr, fs, fr, hs, hr, rs, rr, osem,
+    nt, chunks, lag, lead, early, early_heads, relayed,
+    shifts, q_hbm, k_hbm, v_hbm, cw_hbm, w_hbm, out_hbm, part_hbm,
+    q, kv, hb, asm, mo, mixed, ob, vext, colbias, same, rb, w, acc, cw,
+    lsem, zs, zr, asend, arecv, ms, mr, fs, fr, hs, hr, rs, rr, osem, psem,
 ):
     t = lax.axis_index("tm")
     h = lax.axis_index("height")
@@ -44,8 +46,10 @@
         pltpu.make_async_copy(k_hbm, kv.at[0, 1:3], lsem.at[0]),
         pltpu.make_async_copy(v_hbm, kv.at[1, 1:3], lsem.at[1]),
         pltpu.make_async_copy(q_hbm, q, lsem.at[2]),
+        pltpu.make_async_copy(cw_hbm, cw, lsem.at[3]),
+        pltpu.make_async_copy(w_hbm.at[0 : 2 * GROUP], w, lsem.at[4]),
     ]
-    for load in loads:
+    for load in loads if early_heads else loads[:4]:
         load.start()
 
     greet = [(None, dev) for dev in (nxt, prv, buddy, across)]
@@ -173,23 +177,33 @@
     def _(g):
         asm_copy(0, g).start()
 
-    @pl.loop(0, chunks + lag)
-    def _(i):
+    def z_issue(i):
         @pl.when(i < chunks)
         def _():
             for way in range(2):
                 for tensor in range(2):
                     z_start(0, way, tensor, i)
 
-        @pl.when(i >= lag)
+        @pl.when((i >= lag) & (i < chunks + lag))
         def _():
             for way in range(2):
                 for tensor in range(2):
                     z_start(1, way, tensor, i - lag)
 
-    @pl.loop(0, chunks)
+    def pack_and_send(part, g):
+        asm_copy(part, g).wait_recv()
+        assemble(part, g)
+        x_copy(part, g).start()
+
+    @pl.loop(0, lead)
     def _(g):
+        z_issue(g)
+        pack_and_send(0, g)
         halo_copy(0, g).start()
+
+    @pl.loop(lead, chunks + lag)
+    def _(i):
+        z_issue(i)
 
     qi = lax.broadcasted_iota(jnp.int32, (128, 256), 0)
     ki = lax.broadcasted_iota(jnp.int32, (128, 256), 1)
@@ -200,16 +214,10 @@
     k_low = (ki % 128 // 16 >= s_row).astype(jnp.int32)
     same[...] = (q_low == k_low).astype(jnp.float32)
 
-    def pack_and_send(part, g):
-        asm_copy(part, g).wait_recv()
-        assemble(part, g)
-        x_copy(part, g).start()
-
-    @pl.loop(0, lead)
-    def _(g):
-        pack_and_send(0, g)
-
     loads[2].wait()
+    loads[3].wait()
+    if early_heads:
+        loads[4].wait()
 
     low = [s_row <= j for j in range(8)]
 
@@ -234,29 +242,38 @@
     def dot(a, b):
         return jnp.dot(a, b, preferred_element_type=jnp.float32)
 
-    def attend(frame, lanes):
-        frames = (0, 1) if frame == 0 else (2, 3)
-
-        def keys(ref, tensor, rows):
+    def attend(lanes):
+        pick = same[...] > 0.5
+        pairs = ((0, 1), (2, 3))
+
+        def keys(ref, tensor, rows, frames):
             return jnp.concatenate([x for f in frames for x in slots(ref, (tensor, f), rows, lanes)], axis=0)
 
-        q_one = jnp.concatenate(slots(q, (frame,), r_one, lanes), axis=0)
-        e, inv = weights_of(dot_t(q_one, keys(kv, 0, r_one)))
-        one = (dot(e.astype(jnp.bfloat16), keys(kv, 1, r_one)) * inv).astype(jnp.bfloat16)
-
-        q_two = jnp.concatenate(slots(q, (frame,), r_two, lanes), axis=0)
-        pick = same[...] > 0.5
-        e, inv = weights_of(
-            jnp.where(pick, dot_t(q_two, keys(kv, 0, r_two)), dot_t(q_two, keys(hb, 0, r_halo)))
-        )
-        near = jnp.where(pick, e, 0.0).astype(jnp.bfloat16)
-        far = jnp.where(pick, 0.0, e).astype(jnp.bfloat16)
-        two = ((dot(near, keys(kv, 1, r_two)) + dot(far, keys(hb, 1, r_halo))) * inv).astype(jnp.bfloat16)
-        for j in range(8):
-            a = one[16 * j : 16 * j + 16]
-            b = two[16 * j : 16 * j + 16]
-            ob[frame, j] = jnp.where(low[j], a, b)
-            ob[frame, 8 + j] = jnp.where(low[j], b, a)
+        def queries(frame, rows):
+            return jnp.concatenate(slots(q, (frame,), rows, lanes), axis=0)
+
+        scores_one = [dot_t(queries(f, r_one), keys(kv, 0, r_one, pairs[f])) for f in range(2)]
+        scores_two = []
+        for f in range(2):
+            q_two = queries(f, r_two)
+            scores_two.append(
+                jnp.where(pick, dot_t(q_two, keys(kv, 0, r_two, pairs[f])), dot_t(q_two, keys(hb, 0, r_halo, pairs[f])))
+            )
+        soft = [weights_of(x) for x in scores_one + scores_two]
+        for f in range(2):
+            e, inv = soft[f]
+            one = (dot(e.astype(jnp.bfloat16), keys(kv, 1, r_one, pairs[f])) * inv).astype(jnp.bfloat16)
+            e, inv = soft[2 + f]
+            near = jnp.where(pick, e, 0.0).astype(jnp.bfloat16)
+            far = jnp.where(pick, 0.0, e).astype(jnp.bfloat16)
+            two = (
+                (dot(near, keys(kv, 1, r_two, pairs[f])) + dot(far, keys(hb, 1, r_halo, pairs[f]))) * inv
+            ).astype(jnp.bfloat16)
+            for j in range(8):
+                a = one[16 * j : 16 * j + 16]
+                b = two[16 * j : 16 * j + 16]
+                ob[f, j] = jnp.where(low[j], a, b)
+                ob[f, 8 + j] = jnp.where(low[j], b, a)
 
     def convolve(lanes, mixed_lanes):
         keep_frame = (t > 0, None, None, t < nt - 1)
@@ -291,7 +308,36 @@
                 mixed[f, pl.ds(4 * rb, 4), :, mixed_lanes] = (win + term).astype(jnp.bfloat16)
 
     def out_copy(g):
-        return pltpu.make_async_copy(mixed.at[:, :, :, lanes_of(g)], out_hbm.at[:, :, :, lanes_of(g)], osem.at[g])
+        rest = pl.ds(pl.multiple_of((g - early_heads) * HEAD_DIM, HEAD_DIM), HEAD_DIM)
+        return pltpu.make_async_copy(mixed.at[:, :, :, lanes_of(g)], out_hbm.at[:, :, :, rest], osem.at[g])
+
+    third = acc.shape[1] // 3
+
+    def part_copy(k):
+        cols = pl.ds(pl.multiple_of(k * third, 128), third)
+        return pltpu.make_async_copy(acc.at[:, cols], part_hbm.at[:, cols], psem.at[k])
+
+    def project_early(unit):
+        group, k = unit // 3, unit % 3
+        lanes = pl.ds(pl.multiple_of(group * GROUP, GROUP), GROUP)
+        left = mixed[:, :, :, lanes].reshape(512, GROUP)
+
+        @pl.loop(0, third // TILE)
+        def _(i):
+            cols = pl.ds(pl.multiple_of(k * third + i * TILE, 128), TILE)
+            part = dot(left, w[lanes, cols])
+
+            @pl.when(group == 0)
+            def _():
+                acc[:, cols] = part
+
+            @pl.when(group == 1)
+            def _():
+                acc[:, cols] = acc[:, cols] + part
+
+        @pl.when(group == 1)
+        def _():
+            part_copy(k).start()
 
     for i in range(early):
         relay_step(0, i)
@@ -330,6 +376,7 @@
         @pl.when(i + lead < chunks)
         def _():
             pack_and_send(0, i + lead)
+            halo_copy(0, i + lead).start()
 
         @pl.when((i >= 2) & (i < chunks + 2))
         def _():
@@ -353,10 +400,17 @@
             for part in range(3):
                 halo_copy(part, g).wait_recv()
                 fwd_copy(part, g).wait_recv()
-            for frame in range(2):
-                attend(frame, lanes_of(g))
+            attend(lanes_of(g))
             convolve(lanes_of(g), lanes_of(g))
-            out_copy(g).start()
+
+            @pl.when(g >= early_heads)
+            def _():
+                out_copy(g).start()
+
+        if early_heads:
+            @pl.when((i >= 7) & (i < 13))
+            def _():
+                project_early(i - 7)
 
     @pl.loop(0, chunks)
     def _(g):
@@ -374,7 +428,28 @@
             x_copy(part, g).wait_send()
             fwd_copy(part, g).wait_send()
             halo_copy(part, g).wait_send()
-        out_copy(g).wait()
+
+        @pl.when(g >= early_heads)
+        def _():
+            out_copy(g).wait()
+
+    if early_heads:
+        for k in range(3):
+            part_copy(k).wait()
+
+
+def project_late(first_row, late, tiles, x, w, part, out_hbm, out, osem):
+    def store(i):
+        cols = pl.ds(i * TILE, TILE)
+        return pltpu.make_async_copy(out.at[:, cols], out_hbm.at[:, cols], osem.at[i])
+
+    for i in range(tiles):
+        cols = pl.ds(i * TILE, TILE)
+        late_part = jnp.dot(x[...], w[first_row : first_row + late, cols], preferred_element_type=jnp.float32)
+        out[:, cols] = (part[:, cols] + late_part).astype(jnp.bfloat16)
+        store(i).start()
+    for i in range(tiles):
+        store(i).wait()
 
 
 def body(nt, query_states, key_states, value_states, shifts, conv_kernel, out_weight):
@@ -388,15 +463,24 @@
     any_spec = pl.BlockSpec(memory_space=pl.ANY)
     dma = pltpu.SemaphoreType.DMA
     bf16 = jnp.bfloat16
-    mixed = pl.pallas_call(
-        functools.partial(kernel, nt, heads, lag, lead, early, relayed),
-        out_shape=jax.ShapeDtypeStruct((frames, rows, cols, channels), bf16),
+    early_heads = 8 if heads == 12 else 0
+    late = channels - early_heads * HEAD_DIM
+    tokens = frames * rows * cols
+    operands = [
+        pltpu.with_memory_space_constraint(a, pltpu.HBM)
+        for a in (shifts, query_states, key_states, value_states, conv_kernel, out_weight)
+    ]
+    mixed, part = pl.pallas_call(
+        functools.partial(kernel, nt, heads, lag, lead, early, early_heads, relayed),
+        out_shape=(
+            jax.ShapeDtypeStruct((frames, rows, cols, late), bf16),
+            jax.ShapeDtypeStruct((tokens, width), jnp.float32),
+        ),
         in_specs=[
             pl.BlockSpec(memory_space=pltpu.SMEM),
-            any_spec, any_spec, any_spec,
-            pl.BlockSpec(memory_space=pltpu.VMEM),
+            any_spec, any_spec, any_spec, any_spec, any_spec,
         ],
-        out_specs=any_spec,
+        out_specs=(any_spec, any_spec),
         scratch_shapes=[
             pltpu.VMEM((2, 16, 16, channels), bf16),
             pltpu.VMEM((2, 4, 16, 16, channels), bf16),
@@ -409,7 +493,10 @@
             pltpu.VMEM((128, 256), jnp.float32),
             pltpu.VMEM((128, 256), jnp.float32),
             pltpu.VMEM((max(1, heads // 3), 2, 2, 8, 16, HEAD_DIM), bf16),
-            dma((3,)),
+            pltpu.VMEM((early_heads * HEAD_DIM or 16, width), bf16),
+            pltpu.VMEM((tokens, width if early_heads else 384), jnp.float32),
+            pltpu.VMEM((27, channels), jnp.float32),
+            dma((5,)),
             dma((2, 2, 2, heads)), dma((2, 2, 2, heads)),
             dma((3, heads)), dma((3, heads)),
             dma((3, heads)), dma((3, heads)),
@@ -417,16 +504,29 @@
             dma((3, heads)), dma((3, heads)),
             dma((max(1, heads // 3), 2, 2)), dma((max(1, heads // 3), 2, 2)),
             dma((heads,)),
+            dma((3,)),
         ],
         compiler_params=pltpu.CompilerParams(
-            collective_id=0, has_side_effects=True, vmem_limit_bytes=60 * 2**20
+            collective_id=0, has_side_effects=True, vmem_limit_bytes=40 * 2**20
         ),
         name="window_block",
-    )(shifts, query_states, key_states, value_states, conv_kernel)
-    block_out = jnp.dot(
-        mixed.reshape(frames * rows * cols, channels), out_weight, preferred_element_type=jnp.float32
-    )
-    return block_out.astype(bf16).reshape(frames, rows, cols, width)
+    )(*operands)
+    if not early_heads:
+        block_out = jnp.dot(
+            mixed.reshape(tokens, channels), out_weight, preferred_element_type=jnp.float32
+        )
+        return block_out.astype(bf16).reshape(frames, rows, cols, width)
+    tiles = width // TILE
+    block_out = pl.pallas_call(
+        functools.partial(project_late, early_heads * HEAD_DIM, late, tiles),
+        out_shape=jax.ShapeDtypeStruct((tokens, width), bf16),
+        in_specs=[pl.BlockSpec(memory_space=pltpu.VMEM)] * 3,
+        out_specs=any_spec,
+        scratch_shapes=[pltpu.VMEM((tokens, width), bf16), dma((tiles,))],
+        compiler_params=pltpu.CompilerParams(vmem_limit_bytes=8 * 2**20),
+        name="project_late",
+    )(mixed.reshape(tokens, late), out_weight, part)
+    return block_out.reshape(frames, rows, cols, width)
 
 
 def solution(mesh):

time: 82.4 us -> 76.5 us (0.928)
  matrix products: 9.22 us -> 0 us
  Pallas kernels: 71.9 us -> 75.2 us
    dot_general x1 -> x0, matrix products: 9.22 us -> none  [body(): jnp.dot(mixed.reshape(frames * rows * cols, channels), out_weight, prefer...]
    pallas_call x1 -> x2, Pallas kernels: 71.9 us -> 75.2 us  [the longest x1 72.6 us: body(): pl.pallas_call(functools.partial(kernel, nt, heads, lag, lead, early, ear...]
where the time goes in v3:
time: 76.5 us; the launch traced here: 75.2 us
  Pallas kernels  75.2 us (98%)
    pallas_call x1, Pallas kernels, body(): pl.pallas_call(functools.partial(kernel, nt, heads, lag, lead, early, ear...  72.6 us
    pallas_call x1, Pallas kernels, body(): pl.pallas_call(functools.partial(project_late, early_heads * HEAD_DIM, la...  2.65 us

profile of v3, /device:TPU:1, one launch (start us, length us, event | category | flops | bytes accessed | tf_op | source)
XLA Modules:
  0.0 75.2 jit_solution(15264053999946371115)
XLA Ops:
  0.0 0.0 copy-start
  0.0 72.6 %window_block.1 = (bf16[2,16,16,512]{3,2,1,0:T(8,128)(2,1)S(1)}, f32[512,3072]{1,0:T(8,128)S(1)}) custom-call(s32[2]{0:T(128)} %shifts.1, bf16[2,16,16,1536]{3,2,1,0:T(8,128)(2,1)} %q_hbm.1, bf16[2,16,16,1536]{3,2,1,0:T(8,128)(2,1)} %k_hbm.1, bf16[2,16,16,1536]{3,2,1,0:T(8,128)(2,1)} %v_hbm.1, f32[27,1536]{1,0:T(8,128)} %cw_hbm.1, bf16[1536,3072]{1,0:T(8,128)(2,1)} %w.1), custom_call_target="tpu_custom_call" | custom-call | tf_op jit(solution)/shard_map/window_block/pallas_call | solution.py:473
  72.6 0.0 copy-done
  72.6 2.7 %project_late.1 = bf16[512,3072]{1,0:T(8,128)(2,1)} custom-call(bf16[512,512]{1,0:T(8,128)(2,1)S(1)} %bitcast.2, bf16[1536,3072]{1,0:T(8,128)(2,1)S(1)} %copy-done, f32[512,3072]{1,0:T(8,128)S(1)} %get-tuple-element.8.part), custom_call_target="tpu_custom_call" | custom-call | tf_op jit(solution)/shard_map/project_late/pallas_call | solution.py:520
Async XLA Ops:
  0.0 72.6 %copy-start = (bf16[1536,3072]{1,0:T(8,128)(2,1)S(1)}, bf16[1536,3072]{1,0:T(8,128)(2,1)}, u32[]{:S(2)}) copy-start(bf16[1536,3072]{1,0:T(8,128)(2,1)} %w.1) | copy-start | bytes 28311556

commit v4 on v3

--- a/solution.py
+++ b/solution.py
@@ -13,14 +13,15 @@
 NEG = -1e30
 GROUP = 4 * HEAD_DIM
 TILE = 512
+SIDE_FROM = 4
 SCALE = math.log2(math.e) / math.sqrt(HEAD_DIM)
 
 
 def kernel(
-    nt, chunks, lag, lead, early, early_heads, relayed,
+    nt, chunks, lag, own_lag, lead, early_heads, relayed,
     shifts, q_hbm, k_hbm, v_hbm, cw_hbm, w_hbm, out_hbm, part_hbm,
     q, kv, hb, asm, mo, mixed, ob, vext, colbias, same, rb, w, acc, cw,
-    lsem, zs, zr, asend, arecv, ms, mr, fs, fr, hs, hr, rs, rr, osem, psem,
+    lsem, zs, zr, asend, arecv, ms, mr, fs, fr, hs, hr, rs, rr, cs, osem, psem,
 ):
     t = lax.axis_index("tm")
     h = lax.axis_index("height")
@@ -75,6 +76,14 @@
         greet.append((relay_down, (base, h)))
         greet.append((relay_down, (other + half - 1, h)))
 
+    def side_in(part, g):
+        if not relayed:
+            return False
+        return (t % nz == (nz - 1 if part == 1 else 0)) & (g >= SIDE_FROM)
+
+    def side_out(way, g):
+        return (t % nz == (nz - 2 if way == 0 else 1)) & (g >= SIDE_FROM)
+
     bar = pltpu.get_barrier_semaphore()
     met = 0
     for cond, dev in greet:
@@ -90,50 +99,49 @@
 
     part_frames = (pl.ds(1, 2), pl.ds(0, 1), pl.ds(3, 1))
 
-    def z_copy(phase, way, tensor, g):
+    def z_copy(phase, way, g):
         rows = (m_rows, h_rows)[phase]
-        src = (k_hbm, v_hbm)[tensor].at[1 - way, rows, :, lanes_of(g)]
-        dst = kv.at[tensor, 3 * way, rows, :, lanes_of(g)]
-        return remote(src, dst, zs.at[phase, way, tensor, g], zr.at[phase, way, tensor, g], (nxt, prv)[way])
-
-    def z_start(phase, way, tensor, g):
+        return remote(
+            kv.at[:, 2 - way, rows, :, lanes_of(g)], kv.at[:, 3 * way, rows, :, lanes_of(g)],
+            zs.at[phase, way, g], zr.at[phase, way, g], (nxt, prv)[way],
+        )
+
+    def z_start(phase, way, g):
         if not relayed:
-            z_copy(phase, way, tensor, g).start()
+            z_copy(phase, way, g).start()
             return
-        p = g % 3
+        p = (g + 0) % 3
         detour = (last, first)[way] & (p > 0)
 
         @pl.when(detour)
         def _():
             rows = (m_rows, h_rows)[phase]
-            src = (k_hbm, v_hbm)[tensor].at[1 - way, rows, :, lanes_of(g)]
             remote(
-                src, rb.at[g // 3, phase, tensor], zs.at[phase, way, tensor, g], rr.at[g // 3, phase, tensor],
-                (base + nz * p + (0, nz - 1)[way], h),
+                kv.at[:, 2 - way, rows, :, lanes_of(g)], rb.at[g // 3, phase],
+                zs.at[phase, way, g], rr.at[g // 3, phase], (base + nz * p + (0, nz - 1)[way], h),
             ).start()
 
         @pl.when(jnp.logical_not(detour))
         def _():
-            z_copy(phase, way, tensor, g).start()
-
-    def relay_copy(phase, tensor, g):
+            z_copy(phase, way, g).start()
+
+    def relay_copy(phase, g):
         rows = (m_rows, h_rows)[phase]
         return remote(
-            rb.at[g // 3, phase, tensor], kv.at[tensor, 3 * slot_way, rows, :, lanes_of(g)],
-            rs.at[g // 3, phase, tensor], zr.at[phase, slot_way, tensor, g], (target, h),
-        )
-
-    def relay_incoming(phase, tensor, g):
-        slot = rb.at[g // 3, phase, tensor]
-        return remote(slot, slot, rs.at[g // 3, phase, tensor], rr.at[g // 3, phase, tensor], (target, h))
+            rb.at[g // 3, phase], kv.at[:, 3 * slot_way, rows, :, lanes_of(g)],
+            rs.at[g // 3, phase], zr.at[phase, slot_way, g], (target, h),
+        )
+
+    def relay_incoming(phase, g):
+        slot = rb.at[g // 3, phase]
+        return remote(slot, slot, rs.at[g // 3, phase], rr.at[g // 3, phase], (target, h))
 
     def relay_step(phase, g):
         if relayed:
-            @pl.when(relay & (g % 3 == y))
-            def _():
-                for tensor in range(2):
-                    relay_incoming(phase, tensor, g).wait_recv()
-                    relay_copy(phase, tensor, g).start()
+            @pl.when(relay & ((g + 0) % 3 == y))
+            def _():
+                relay_incoming(phase, g).wait_recv()
+                relay_copy(phase, g).start()
 
     def asm_copy(part, g):
         fr_ = part_frames[part]
@@ -147,6 +155,12 @@
         return remote(
             mo.at[fr_, :, :, lanes_of(g)], hb.at[core, fr_, 0:8, :, lanes_of(g)],
             ms.at[part, g], mr.at[part, g], across,
+        )
+
+    def side_copy(way, g):
+        return remote(
+            hb.at[core, pl.ds(2 - way, 1), 0:8, :, lanes_of(g)], hb.at[core, pl.ds(3 * way, 1), 0:8, :, lanes_of(g)],
+            cs.at[way, g], mr.at[1 + way, g], (nxt, prv)[way],
         )
 
     def fwd_copy(part, g):
@@ -181,19 +195,23 @@
         @pl.when(i < chunks)
         def _():
             for way in range(2):
-                for tensor in range(2):
-                    z_start(0, way, tensor, i)
+                z_start(0, way, i)
 
         @pl.when((i >= lag) & (i < chunks + lag))
         def _():
             for way in range(2):
-                for tensor in range(2):
-                    z_start(1, way, tensor, i - lag)
+                z_start(1, way, i - lag)
 
     def pack_and_send(part, g):
         asm_copy(part, g).wait_recv()
-        assemble(part, g)
-        x_copy(part, g).start()
+        if part == 0 or not relayed:
+            assemble(part, g)
+            x_copy(part, g).start()
+        else:
+            @pl.when(jnp.logical_not(side_in(part, g)))
+            def _():
+                assemble(part, g)
+                x_copy(part, g).start()
 
     @pl.loop(0, lead)
     def _(g):
@@ -339,34 +357,63 @@
         def _():
             part_copy(k).start()
 
-    for i in range(early):
-        relay_step(0, i)
-        if i >= lag:
-            relay_step(1, i - lag)
-
-    @pl.loop(0, chunks + 3)
+    def settle(g):
+        for phase in range(2):
+            for way in range(2):
+                z_copy(phase, way, g).wait_send()
+            if relayed:
+                @pl.when(relay & ((g + 0) % 3 == y))
+                def _():
+                    relay_copy(phase, g).wait_send()
+        for part in range(3):
+            asm_copy(part, g).wait_send()
+            if part == 0 or not relayed:
+                x_copy(part, g).wait_send()
+            else:
+                @pl.when(jnp.logical_not(side_in(part, g)))
+                def _():
+                    x_copy(part, g).wait_send()
+
+                @pl.when(side_out(part - 1, g))
+                def _():
+                    side_copy(part - 1, g).wait_send()
+            fwd_copy(part, g).wait_send()
+            halo_copy(part, g).wait_send()
+
+        @pl.when(g >= early_heads)
+        def _():
+            out_copy(g).wait()
+
+    @pl.loop(0, chunks + lag + 1)
     def _(i):
-        @pl.when(i + early < chunks)
-        def _():
-            relay_step(0, i + early)
-
-        @pl.when((i + early >= lag) & (i + early < chunks + lag))
-        def _():
-            relay_step(1, i + early - lag)
+        for more in range(2):
+            v = (3 * i + 1) // 2 + more
+
+            @pl.when((2 * v // 3 == i) & (v < chunks))
+            def _():
+                relay_step(0, v)
+
+            @pl.when((2 * v // 3 == i) & (v >= lag) & (v < chunks + lag))
+            def _():
+                relay_step(1, v - lag)
 
         @pl.when(i < chunks)
         def _():
             for way in range(2):
-                for tensor in range(2):
-                    z_copy(0, way, tensor, i).wait_recv()
+                z_copy(0, way, i).wait_recv()
             for part in (1, 2):
                 asm_copy(part, i).start()
 
-        @pl.when((i >= 2) & (i < chunks + 2))
-        def _():
-            g = i - 2
+        @pl.when((i >= own_lag) & (i < chunks + own_lag))
+        def _():
+            g = i - own_lag
             x_copy(0, g).wait_recv()
             fwd_copy(0, g).start()
+            if relayed:
+                for way in range(2):
+                    @pl.when(side_out(way, g))
+                    def _():
+                        side_copy(way, g).start()
 
         @pl.when((i >= 1) & (i < chunks + 1))
         def _():
@@ -378,25 +425,24 @@
             pack_and_send(0, i + lead)
             halo_copy(0, i + lead).start()
 
-        @pl.when((i >= 2) & (i < chunks + 2))
-        def _():
-            g = i - 2
+        @pl.when((i >= lag) & (i < chunks + lag))
+        def _():
+            g = i - lag
             for way in range(2):
-                for tensor in range(2):
-                    z_copy(1, way, tensor, g).wait_recv()
+                z_copy(1, way, g).wait_recv()
             for part in (1, 2):
                 halo_copy(part, g).start()
 
-        @pl.when((i >= 2) & (i < chunks + 2))
-        def _():
-            g = i - 2
+        @pl.when((i >= lag) & (i < chunks + lag))
+        def _():
+            g = i - lag
             for part in (1, 2):
                 x_copy(part, g).wait_recv()
                 fwd_copy(part, g).start()
 
-        @pl.when(i >= 3)
-        def _():
-            g = i - 3
+        @pl.when(i > lag)
+        def _():
+            g = i - lag - 1
             for part in range(3):
                 halo_copy(part, g).wait_recv()
                 fwd_copy(part, g).wait_recv()
@@ -408,30 +454,20 @@
                 out_copy(g).start()
 
         if early_heads:
-            @pl.when((i >= 7) & (i < 13))
-            def _():
-                project_early(i - 7)
-
-    @pl.loop(0, chunks)
+            for group in range(2):
+                first_step = lag + 4 + 4 * group
+
+                @pl.when((i >= first_step) & (i < first_step + 3))
+                def _():
+                    project_early(3 * group + i - first_step)
+
+        @pl.when(i > lag + 3)
+        def _():
+            settle(i - lag - 4)
+
+    @pl.loop(max(0, chunks - 3), chunks)
     def _(g):
-        for phase in range(2):
-            for way in range(2):
-                for tensor in range(2):
-                    z_copy(phase, way, tensor, g).wait_send()
-            if relayed:
-                @pl.when(relay & (g % 3 == y))
-                def _():
-                    for tensor in range(2):
-                        relay_copy(phase, tensor, g).wait_send()
-        for part in range(3):
-            asm_copy(part, g).wait_send()
-            x_copy(part, g).wait_send()
-            fwd_copy(part, g).wait_send()
-            halo_copy(part, g).wait_send()
-
-        @pl.when(g >= early_heads)
-        def _():
-            out_copy(g).wait()
+        settle(g)
 
     if early_heads:
         for k in range(3):
@@ -456,8 +492,8 @@
     frames, rows, cols, channels = query_states.shape
     width = out_weight.shape[1]
     heads = channels // HEAD_DIM
-    lag = 2
-    early = 2
+    lag = min(4, heads)
+    own_lag = min(2, heads)
     lead = min(4, heads)
     relayed = nt == 64 and heads % 3 == 0
     any_spec = pl.BlockSpec(memory_space=pl.ANY)
@@ -471,7 +507,7 @@
         for a in (shifts, query_states, key_states, value_states, conv_kernel, out_weight)
     ]
     mixed, part = pl.pallas_call(
-        functools.partial(kernel, nt, heads, lag, lead, early, early_heads, relayed),
+        functools.partial(kernel, nt, heads, lag, own_lag, lead, early_heads, relayed),
         out_shape=(
             jax.ShapeDtypeStruct((frames, rows, cols, late), bf16),
             jax.ShapeDtypeStruct((tokens, width), jnp.float32),
@@ -497,12 +533,13 @@
             pltpu.VMEM((tokens, width if early_heads else 384), jnp.float32),
             pltpu.VMEM((27, channels), jnp.float32),
             dma((5,)),
-            dma((2, 2, 2, heads)), dma((2, 2, 2, heads)),
+            dma((2, 2, heads)), dma((2, 2, heads)),
             dma((3, heads)), dma((3, heads)),
             dma((3, heads)), dma((3, heads)),
             dma((3, heads)), dma((3, heads)),
             dma((3, heads)), dma((3, heads)),
-            dma((max(1, heads // 3), 2, 2)), dma((max(1, heads // 3), 2, 2)),
+            dma((max(1, heads // 3), 2)), dma((max(1, heads // 3), 2)),
+            dma((2, heads)),
             dma((heads,)),
             dma((3,)),
         ],

time: 76.5 us -> 71.5 us (0.935)
  Pallas kernels: 75.2 us -> 70.8 us
    pallas_call x1, Pallas kernels: 72.6 us -> 68.1 us  [body(): pl.pallas_call(functools.partial(kernel, nt, heads, lag, own_lag, lead, e...]
where the time goes in v4:
time: 71.5 us; the launch traced here: 70.8 us
  Pallas kernels  70.8 us (99%)
    pallas_call x1, Pallas kernels, body(): pl.pallas_call(functools.partial(kernel, nt, heads, lag, own_lag, lead, e...  68.1 us
    pallas_call x1, Pallas kernels, body(): pl.pallas_call(functools.partial(project_late, early_heads * HEAD_DIM, la...  2.65 us

profile of v4, /device:TPU:1, one launch (start us, length us, event | category | flops | bytes accessed | tf_op | source)
XLA Modules:
  0.0 70.8 jit_solution(11536532122326557010)
XLA Ops:
  0.0 0.0 copy-start
  0.0 68.1 %window_block.1 = (bf16[2,16,16,512]{3,2,1,0:T(8,128)(2,1)S(1)}, f32[512,3072]{1,0:T(8,128)S(1)}) custom-call(s32[2]{0:T(128)} %shifts.1, bf16[2,16,16,1536]{3,2,1,0:T(8,128)(2,1)} %q_hbm.1, bf16[2,16,16,1536]{3,2,1,0:T(8,128)(2,1)} %k_hbm.1, bf16[2,16,16,1536]{3,2,1,0:T(8,128)(2,1)} %v_hbm.1, f32[27,1536]{1,0:T(8,128)} %cw_hbm.1, bf16[1536,3072]{1,0:T(8,128)(2,1)} %w.1), custom_call_target="tpu_custom_call" | custom-call | tf_op jit(solution)/shard_map/window_block/pallas_call | solution.py:509
  68.1 0.0 copy-done
  68.2 2.7 %project_late.1 = bf16[512,3072]{1,0:T(8,128)(2,1)} custom-call(bf16[512,512]{1,0:T(8,128)(2,1)S(1)} %bitcast.2, bf16[1536,3072]{1,0:T(8,128)(2,1)S(1)} %copy-done, f32[512,3072]{1,0:T(8,128)S(1)} %get-tuple-element.8.part), custom_call_target="tpu_custom_call" | custom-call | tf_op jit(solution)/shard_map/project_late/pallas_call | solution.py:557
Async XLA Ops:
  0.0 68.1 %copy-start = (bf16[1536,3072]{1,0:T(8,128)(2,1)S(1)}, bf16[1536,3072]{1,0:T(8,128)(2,1)}, u32[]{:S(2)}) copy-start(bf16[1536,3072]{1,0:T(8,128)(2,1)} %w.1) | copy-start | bytes 28311556

commit v5 on v4

--- a/solution.py
+++ b/solution.py
@@ -219,9 +219,16 @@
         pack_and_send(0, g)
         halo_copy(0, g).start()
 
-    @pl.loop(lead, chunks + lag)
-    def _(i):
-        z_issue(i)
+    paced = False
+    if relayed:
+        paced = (t % nz == 1) | (t % nz == nz - 2)
+
+    @pl.when(jnp.logical_not(paced))
+    def _():
+        @pl.loop(lead, chunks + lag)
+        def _(i):
+            z_issue(i)
+
 
     qi = lax.broadcasted_iota(jnp.int32, (128, 256), 0)
     ki = lax.broadcasted_iota(jnp.int32, (128, 256), 1)
@@ -419,6 +426,10 @@
         def _():
             for part in (1, 2):
                 pack_and_send(part, i - 1)
+
+        @pl.when(paced & (i + lead < chunks + lag))
+        def _():
+            z_issue(i + lead)
 
         @pl.when(i + lead < chunks)
         def _():

time: 71.5 us -> 71.6 us (level)
  no operation moved by 1% of the time
where the time goes in v5:
time: 71.6 us; the launch traced here: 70.9 us
  Pallas kernels  70.8 us (99%)
    pallas_call x1, Pallas kernels, body(): pl.pallas_call(functools.partial(kernel, nt, heads, lag, own_lag, lead, e...  68.2 us
    pallas_call x1, Pallas kernels, body(): pl.pallas_call(functools.partial(project_late, early_heads * HEAD_DIM, la...  2.65 us

profile of v5, /device:TPU:1, one launch (start us, length us, event | category | flops | bytes accessed | tf_op | source)
XLA Modules:
  0.0 70.9 jit_solution(12589962503344349787)
XLA Ops:
  0.0 0.0 copy-start
  0.0 68.2 %window_block.1 = (bf16[2,16,16,512]{3,2,1,0:T(8,128)(2,1)S(1)}, f32[512,3072]{1,0:T(8,128)S(1)}) custom-call(s32[2]{0:T(128)} %shifts.1, bf16[2,16,16,1536]{3,2,1,0:T(8,128)(2,1)} %q_hbm.1, bf16[2,16,16,1536]{3,2,1,0:T(8,128)(2,1)} %k_hbm.1, bf16[2,16,16,1536]{3,2,1,0:T(8,128)(2,1)} %v_hbm.1, f32[27,1536]{1,0:T(8,128)} %cw_hbm.1, bf16[1536,3072]{1,0:T(8,128)(2,1)} %w.1), custom_call_target="tpu_custom_call" | custom-call | tf_op jit(solution)/shard_map/window_block/pallas_call | solution.py:520
  68.2 0.0 copy-done
  68.2 2.7 %project_late.1 = bf16[512,3072]{1,0:T(8,128)(2,1)} custom-call(bf16[512,512]{1,0:T(8,128)(2,1)S(1)} %bitcast.2, bf16[1536,3072]{1,0:T(8,128)(2,1)S(1)} %copy-done, f32[512,3072]{1,0:T(8,128)S(1)} %get-tuple-element.8.part), custom_call_target="tpu_custom_call" | custom-call | tf_op jit(solution)/shard_map/project_late/pallas_call | solution.py:568
Async XLA Ops:
  0.0 68.2 %copy-start = (bf16[1536,3072]{1,0:T(8,128)(2,1)S(1)}, bf16[1536,3072]{1,0:T(8,128)(2,1)}, u32[]{:S(2)}) copy-start(bf16[1536,3072]{1,0:T(8,128)(2,1)} %w.1) | copy-start | bytes 28311556
